TPU v7x, 128 devices: a whole 4x4x4 slice. The times are simulated.
128 devices in a mesh: seq: 2 (over z_lo), dp: 64 (over y, x, z_hi, core).
Axes of the slice: x: 4, y: 4, z: 4 (z_hi: 2, z_lo: 2; z = z_hi * 2 + z_lo), core: 2. Of those that a mesh axis runs over, the one named last changes fastest.
Arguments:
- layer_input: bfloat16 [64, 512, 1024], P('dp', 'seq'), may hold values from -6 to 6
- segments: int32 [64, 512], P('dp', 'seq'), may hold values from 0 to 1, as said below
- positions: int32 [64, 512], P('dp', 'seq'), may hold values from 0 to 2558, as said below
- qkv_weight: bfloat16 [1024, 4096], P(None, ('seq', 'dp')), may hold values from -0.1875 to 0.1875
- out_weight: bfloat16 [2048, 1024], P(('seq', 'dp')), may hold values from -1 to 1
- mlp_weight: bfloat16 [3072, 3, 1024], P(('seq', 'dp')), may hold values from -0.1875 to 0.1875
- gains: bfloat16 [2304], P(('seq', 'dp')), may hold values from 0.25 to 1.75
- cotangent: bfloat16 [64, 512, 1024], P('dp', 'seq'), may hold values from -6 to 6
Outputs:
- layer_output: bfloat16 [64, 512, 1024], P('dp', 'seq')
- input_grad: bfloat16 [64, 512, 1024], P('dp', 'seq')
- qkv_grad: float32 [1024, 4096], P(None, ('seq', 'dp'))
- out_grad: float32 [2048, 1024], P(('seq', 'dp'))
- mlp_grad: float32 [3072, 3, 1024], P(('seq', 'dp'))
- gains_grad: float32 [2304], P(('seq', 'dp'))
Inputs may be any that keep to these rules, and one draw needn't show every extreme that they name: `segments`: each sequence holds two documents, numbered 0 then 1, each of 128 tokens or more. Within a document positions rise by one from token to token.
All inputs are finite; a program needn't handle non-finite values.
Results may differ from a plain program's by a relative error of at most 0.018.
Values may be sent and summed in bfloat16 or wider, within the bound.
A program may use at most 256 MiB of HBM per device.

v0:
```python
import jax
import jax.numpy as jnp
from jax import lax
from jax.sharding import PartitionSpec as P

HEADS = 16
KV_HEADS = 8
HEAD = 128


EPSILON = 1e-06
THETA_BASE = 1000000.0
MASKED = -1e30


def contract_last(left, right):
    return lax.dot_general(
        left, right, (((1,), (1,)), ((), ())), preferred_element_type=jnp.float32
    )


def contract_first(left, right):
    return lax.dot_general(
        left, right, (((0,), (0,)), ((), ())), preferred_element_type=jnp.float32
    )


def norm_scale(values):
    return lax.rsqrt(jnp.mean(values * values, axis=-1, keepdims=True) + EPSILON)


def norm_back(incoming, values, scale, gain):
    weighted = incoming * gain
    grad_in = scale * weighted - values * scale**3 * jnp.mean(
        weighted * values, axis=-1, keepdims=True
    )
    return (grad_in, incoming * values * scale)


def rope_tables(places):
    half_size = HEAD // 2
    freqs = THETA_BASE ** (-(jnp.arange(half_size, dtype=jnp.float32) * 2.0) / HEAD)
    angles = places.astype(jnp.float32)[..., None] * freqs
    cosine = jnp.concatenate([jnp.cos(angles), jnp.cos(angles)], axis=-1)[..., None, :]
    sine = jnp.concatenate([jnp.sin(angles), jnp.sin(angles)], axis=-1)[..., None, :]
    return (cosine, sine)


def rotate(values, cosine, sine):
    first_half, second_half = jnp.split(values, 2, axis=-1)
    return values * cosine + jnp.concatenate([-second_half, first_half], axis=-1) * sine


def unrotate(incoming, cosine, sine):
    moved = incoming * sine
    first_half, second_half = jnp.split(moved, 2, axis=-1)
    return incoming * cosine + jnp.concatenate([second_half, -first_half], axis=-1)


def shards(layer_input, segments, positions, qkv_weight, out_weight, mlp_weight, gains, cotangent):
    rows_here = layer_input.shape[1]
    model_width = layer_input.shape[2]
    heads_per_kv = HEADS // KV_HEADS
    query_width = HEADS * HEAD
    key_width = KV_HEADS * HEAD
    scale_factor = HEAD ** (-0.5)
    w_qkv, w_out, w_mlp, gain_all = (
        lax.all_gather(qkv_weight, ("seq", "dp"), axis=1, tiled=True),
        lax.all_gather(out_weight, ("seq", "dp"), axis=0, tiled=True),
        lax.all_gather(mlp_weight, ("seq", "dp"), axis=0, tiled=True),
        lax.all_gather(gains, ("seq", "dp"), axis=0, tiled=True),
    )
    gain_full = gain_all.astype(jnp.float32)
    gain_in = gain_full[:model_width]
    gain_mlp = gain_full[model_width : 2 * model_width]
    gain_query = gain_full[2 * model_width : 2 * model_width + HEAD]
    gain_key = gain_full[2 * model_width + HEAD :]
    inputs = layer_input[0].astype(jnp.float32)
    scale_in = norm_scale(inputs)
    input_normed = (inputs * scale_in * gain_in).astype(jnp.bfloat16)
    projected = jnp.dot(input_normed, w_qkv, preferred_element_type=jnp.float32)
    query_pre = projected[:, :query_width].reshape(rows_here, HEADS, HEAD)
    key_pre = projected[:, query_width : query_width + key_width].reshape(rows_here, KV_HEADS, HEAD)
    value_pre = projected[:, query_width + key_width :]
    scale_query = norm_scale(query_pre)
    scale_key = norm_scale(key_pre)
    cosine, sine = rope_tables(positions[0])
    queries = rotate(query_pre * scale_query * gain_query, cosine, sine).astype(jnp.bfloat16)
    keys_here = rotate(key_pre * scale_key * gain_key, cosine, sine).astype(jnp.bfloat16)
    packed = jnp.concatenate(
        [keys_here.reshape(rows_here, key_width), value_pre.astype(jnp.bfloat16)], axis=1
    )
    seg_here = segments[0]
    packed_all, key_segments = (
        lax.all_gather(packed, "seq", axis=0, tiled=True),
        lax.all_gather(seg_here, "seq", axis=0, tiled=True),
    )
    seq_length = key_segments.shape[0]
    keys_all = packed_all[:, :key_width].reshape(seq_length, KV_HEADS, HEAD)
    values_all = packed_all[:, key_width:].reshape(seq_length, KV_HEADS, HEAD)
    query_index = lax.axis_index("seq") * rows_here + jnp.arange(rows_here, dtype=jnp.int32)
    key_index = jnp.arange(seq_length, dtype=jnp.int32)
    allowed = (seg_here[:, None] == key_segments[None, :]) & (
        key_index[None, :] <= query_index[:, None]
    )
    grouped = queries.reshape(rows_here, KV_HEADS, heads_per_kv, HEAD)
    scores = (
        jnp.einsum("tkgd,ukd->kgtu", grouped, keys_all, preferred_element_type=jnp.float32)
        * scale_factor
    )
    scores = jnp.where(allowed[None, None], scores, MASKED)
    exponent = jnp.exp(scores - jnp.max(scores, axis=-1, keepdims=True))
    weights_soft = exponent / jnp.sum(exponent, axis=-1, keepdims=True)
    weights_low = weights_soft.astype(jnp.bfloat16)
    context = jnp.einsum(
        "kgtu,ukd->tkgd", weights_low, values_all, preferred_element_type=jnp.float32
    )
    context = context.reshape(rows_here, query_width).astype(jnp.bfloat16)
    hidden_res = inputs + jnp.dot(context, w_out, preferred_element_type=jnp.float32)
    scale_mlp = norm_scale(hidden_res)
    mlp_in = (hidden_res * scale_mlp * gain_mlp).astype(jnp.bfloat16)
    gate_pre = contract_last(mlp_in, w_mlp[:, 0, :])
    up_pre = contract_last(mlp_in, w_mlp[:, 1, :])
    sigmoid_gate = jax.nn.sigmoid(gate_pre)
    activated = (gate_pre * sigmoid_gate * up_pre).astype(jnp.bfloat16)
    layer_out = hidden_res + jnp.dot(activated, w_mlp[:, 2, :], preferred_element_type=jnp.float32)
    back_qkv, back_out, back_mlp = (
        lax.all_gather(qkv_weight, ("seq", "dp"), axis=1, tiled=True),
        lax.all_gather(out_weight, ("seq", "dp"), axis=0, tiled=True),
        lax.all_gather(mlp_weight, ("seq", "dp"), axis=0, tiled=True),
    )
    grad_out = cotangent[0]
    d_act = contract_last(grad_out, back_mlp[:, 2, :])
    d_gate = (d_act * up_pre * sigmoid_gate * (1.0 + gate_pre * (1.0 - sigmoid_gate))).astype(
        jnp.bfloat16
    )
    d_up = (d_act * gate_pre * sigmoid_gate).astype(jnp.bfloat16)
    mlp_term = jnp.stack(
        [
            contract_first(d_gate, mlp_in),
            contract_first(d_up, mlp_in),
            contract_first(activated, grad_out),
        ],
        axis=1,
    )
    d_mlp_in = jnp.dot(d_gate, back_mlp[:, 0, :], preferred_element_type=jnp.float32) + jnp.dot(
        d_up, back_mlp[:, 1, :], preferred_element_type=jnp.float32
    )
    d_norm_mlp, gain_term_mlp = norm_back(d_mlp_in, hidden_res, scale_mlp, gain_mlp)
    d_hidden = grad_out.astype(jnp.float32) + d_norm_mlp
    d_attn = d_hidden.astype(jnp.bfloat16)
    out_term = contract_first(context, d_attn)
    d_context = (
        contract_last(d_attn, back_out)
        .astype(jnp.bfloat16)
        .reshape(rows_here, KV_HEADS, heads_per_kv, HEAD)
    )
    d_weights = jnp.einsum(
        "tkgd,ukd->kgtu", d_context, values_all, preferred_element_type=jnp.float32
    )
    d_scores = weights_soft * (
        d_weights - jnp.sum(weights_soft * d_weights, axis=-1, keepdims=True)
    )
    d_scores = d_scores.astype(jnp.bfloat16)
    d_queries = jnp.einsum("kgtu,ukd->tkgd", d_scores, keys_all, preferred_element_type=jnp.float32)
    d_queries = d_queries.reshape(rows_here, HEADS, HEAD) * scale_factor
    d_keys_all = (
        jnp.einsum("kgtu,tkgd->ukd", d_scores, grouped, preferred_element_type=jnp.float32)
        * scale_factor
    )
    d_values_all = jnp.einsum(
        "kgtu,tkgd->ukd", weights_low, d_context, preferred_element_type=jnp.float32
    )
    d_packed = jnp.concatenate(
        [d_keys_all.reshape(seq_length, key_width), d_values_all.reshape(seq_length, key_width)],
        axis=1,
    )
    d_packed_own = lax.psum_scatter(
        d_packed.astype(jnp.bfloat16), "seq", scatter_dimension=0, tiled=True
    ).astype(jnp.float32)
    d_keys = d_packed_own[:, :key_width].reshape(rows_here, KV_HEADS, HEAD)
    d_query_pre, gain_term_query = norm_back(
        unrotate(d_queries, cosine, sine), query_pre, scale_query, gain_query
    )
    d_key_pre, gain_term_key = norm_back(
        unrotate(d_keys, cosine, sine), key_pre, scale_key, gain_key
    )
    d_projected = jnp.concatenate(
        [
            d_query_pre.reshape(rows_here, query_width),
            d_key_pre.reshape(rows_here, key_width),
            d_packed_own[:, key_width:],
        ],
        axis=1,
    ).astype(jnp.bfloat16)
    qkv_term = contract_first(input_normed, d_projected)
    d_input_normed = contract_last(d_projected, back_qkv)
    d_norm_in, gain_term_in = norm_back(d_input_normed, inputs, scale_in, gain_in)
    input_grad = (d_hidden + d_norm_in).astype(jnp.bfloat16)
    gain_term = jnp.concatenate(
        [
            jnp.sum(gain_term_in, axis=0),
            jnp.sum(gain_term_mlp, axis=0),
            jnp.sum(gain_term_query, axis=(0, 1)),
            jnp.sum(gain_term_key, axis=(0, 1)),
        ]
    )
    qkv_share, out_share, mlp_share, gain_share = (
        lax.psum_scatter(qkv_term, ("seq", "dp"), scatter_dimension=1, tiled=True),
        lax.psum_scatter(out_term, ("seq", "dp"), scatter_dimension=0, tiled=True),
        lax.psum_scatter(mlp_term, ("seq", "dp"), scatter_dimension=0, tiled=True),
        lax.psum_scatter(gain_term, ("seq", "dp"), scatter_dimension=0, tiled=True),
    )
    return (
        layer_out.astype(jnp.bfloat16)[None],
        input_grad[None],
        qkv_share,
        out_share,
        mlp_share,
        gain_share,
    )


def solution(mesh):
    in_specs = (
        P("dp", "seq", None),
        P("dp", "seq"),
        P("dp", "seq"),
        P(None, ("seq", "dp")),
        P(("seq", "dp"), None),
        P(("seq", "dp"), None, None),
        P(("seq", "dp")),
        P("dp", "seq", None),
    )
    out_specs = (
        P("dp", "seq", None),
        P("dp", "seq", None),
        P(None, ("seq", "dp")),
        P(("seq", "dp"), None),
        P(("seq", "dp"), None, None),
        P(("seq", "dp")),
    )
    return jax.shard_map(shards, mesh=mesh, in_specs=in_specs, out_specs=out_specs, check_vma=False)
```

profile of v0, /device:TPU:1, one launch (start us, length us, event | category | flops | bytes accessed | tf_op | source)
XLA Modules:
  0.0 2834.1 jit_solution(4920976554879823842)
XLA Ops:
  10.8 68.9 %all-reduce = bf16[2304]{0:T(1024)(128)(2,1)S(1)} all-reduce(bf16[2304]{0:T(1024)(128)(2,1)S(1)} %dynamic-update-slice), channel_id=1, replica_groups=mesh['seq'=2,'dp'=64] {'seq','dp'}, use_global_device_ids=true, to_apply=%add | all-reduce | flops 2304 | bytes 9216
  81.9 133.9 %all-gather.6.cloned.1.call-done = bf16[1024,4096]{0,1:T(8,128)(2,1)} async-done(((bf16[1024,32]{0,1:T(8,128)(2,1)}), bf16[1024,4096]{0,1:T(8,128)(2,1)}) %all-gather.6.cloned.1.call-update) | async-done | bytes 8388624 | tf_op jit(solution)/shard_map/all_gather | solution.py:68
  215.8 6.0 fusion.69
  246.7 18.4 all-gather.8.cloned.1.call-done
  272.2 8.4 fusion.79
  280.6 5.6 fusion.27
  286.2 179.3 %all-gather.10.cloned.1.call-done = bf16[2048,1024]{1,0:T(8,128)(2,1)} async-done(((bf16[16,1024]{1,0:T(8,128)(2,1)}), bf16[2048,1024]{1,0:T(8,128)(2,1)}) %all-gather.10.cloned.1.call-update) | async-done | bytes 4194320 | tf_op jit(solution)/shard_map/all_gather | solution.py:69
  471.6 212.1 %all-gather.12.cloned.1.call-done = bf16[3072,3,1024]{2,0,1:T(8,128)(2,1)} async-done(((bf16[24,3,1024]{2,0,1:T(8,128)(2,1)}), bf16[3072,3,1024]{2,0,1:T(8,128)(2,1)}) %all-gather.12.cloned.1.call-update) | async-done | bytes 18874384 | tf_op jit(solution)/shard_map/all_gather | solution.py:70
  693.3 7.2 multiply_convert_fusion
  700.5 6.0 fusion.5
  706.5 5.6 multiply_reduce_fusion.2
  718.1 6.3 bitcast_convert_fusion
  724.4 6.8 fusion.1
  733.5 6.7 fusion.3
  748.1 6.1 fusion.65
  783.1 8.0 multiply_reduce_fusion
  801.0 8.3 fusion.57
  817.3 12.7 pad_maximum_fusion
  831.8 5.5 fusion.35
  837.4 6.1 fusion.46
  843.5 63.9 %all-reduce.1 = f32[2304]{0:T(1024)S(1)} all-reduce(f32[2304]{0:T(1024)S(1)} %pad_maximum_fusion.10), channel_id=7, replica_groups=mesh['seq'=2,'dp'=64] {'seq','dp'}, use_global_device_ids=true, to_apply=%region_21.22.clone | all-reduce | flops 2304 | bytes 18432
  909.1 519.9 %reduce-scatter.9.cloned.1.call-done = f32[16,1024]{1,0:T(8,128)} async-done(((f32[2048,1024]{1,0:T(8,128)}), f32[16,1024]{1,0:T(8,128)}) %reduce-scatter.9.cloned.1.call-update) | async-done | bytes 65552 | tf_op jit(solution)/shard_map/reduce_scatter | solution.py:210
  1429.0 670.1 %reduce-scatter.7.cloned.1.call-done = f32[1024,32]{0,1:T(8,128)} async-done(((f32[1024,4096]{0,1:T(8,128)}), f32[1024,32]{0,1:T(8,128)}) %reduce-scatter.7.cloned.1.call-update) | async-done | bytes 131088 | tf_op jit(solution)/shard_map/reduce_scatter | solution.py:209
  2099.0 727.8 %reduce-scatter.11.cloned.1.call-done = f32[24,3,1024]{2,0,1:T(8,128)} async-done(((f32[3072,3,1024]{2,0,1:T(8,128)}), f32[24,3,1024]{2,0,1:T(8,128)}) %reduce-scatter.11.cloned.1.call-update) | async-done | bytes 294928 | tf_op jit(solution)/shard_map/reduce_scatter | solution.py:211
  (223 shorter events, 119.4 us)
Async XLA Ops:
  7.2 208.7 %all-gather.6.cloned.1.call-start = ((), (), s32[]{:S(2)}) async-start(), calls=%async_computation.4 | async-start | bytes 8454144 | tf_op jit(solution)/shard_map/all_gather | solution.py:68
  7.9 257.2 %all-gather.8.cloned.1.call-start = ((), (), s32[]{:S(2)}) async-start(), calls=%async_computation.5 | async-start | bytes 3145728 | tf_op jit(solution)/shard_map/all_gather | solution.py:95
  9.6 212.2 %copy-start.32 = (f32[256,128]{0,1:T(8,128)}, f32[256,128]{0,1:T(8,128)S(1)}, u32[]{:S(2)}) copy-start(f32[256,128]{0,1:T(8,128)S(1)} %get-tuple-element.34) | copy-start | bytes 393220
  9.8 212.1 %copy-start.34 = (f32[256,128]{0,1:T(8,128)}, f32[256,128]{0,1:T(8,128)S(1)}, u32[]{:S(2)}) copy-start(f32[256,128]{0,1:T(8,128)S(1)} %get-tuple-element.36) | copy-start | bytes 393220
  81.9 143.3 %copy-start.49 = (f32[128]{0:T(128)}, f32[128]{0:T(128)S(1)}, u32[]{:S(2)}) copy-start(f32[128]{0:T(128)S(1)} %get-tuple-element.44) | copy-start | bytes 1540
  230.3 235.2 %all-gather.10.cloned.1.call-start = ((), (), s32[]{:S(2)}) async-start(), calls=%async_computation.6 | async-start | bytes 4227072 | tf_op jit(solution)/shard_map/all_gather | solution.py:69
  231.1 452.7 %all-gather.12.cloned.1.call-start = ((), (), s32[]{:S(2)}) async-start(), calls=%async_computation.7 | async-start | bytes 19021824 | tf_op jit(solution)/shard_map/all_gather | solution.py:70
  231.7 559.5 %reduce-scatter.5.cloned.1.call-start = ((), (), s32[]{:S(2)}) async-start(), calls=%async_computation.8 | async-start | bytes 3145728 | tf_op jit(solution)/shard_map/reduce_scatter | solution.py:178
  700.5 6.0 copy-start.29
  700.5 6.0 copy-start.31
  700.5 6.0 copy-start.18
  700.5 6.0 copy-start.48
  706.5 5.6 copy-start.53
  706.5 7.0 copy-start.55
  718.1 6.3 copy-start.36
  718.1 6.3 copy-start.37
  718.1 6.3 copy-start.44
  733.5 6.7 copy-start.20
  748.1 680.9 %reduce-scatter.9.cloned.1.call-start = ((), (), s32[]{:S(2)}) async-start(), calls=%async_computation.10 | async-start | bytes 8454144 | tf_op jit(solution)/shard_map/reduce_scatter | solution.py:210
  754.2 1344.8 %reduce-scatter.7.cloned.1.call-start = ((), (), s32[]{:S(2)}) async-start(), calls=%async_computation.9 | async-start | bytes 16908288 | tf_op jit(solution)/shard_map/reduce_scatter | solution.py:209
  809.3 2017.5 %reduce-scatter.11.cloned.1.call-start = ((), (), s32[]{:S(2)}) async-start(), calls=%async_computation.11 | async-start | bytes 38043648 | tf_op jit(solution)/shard_map/reduce_scatter | solution.py:211
  837.4 6.1 copy-start.54
  837.4 70.6 %copy-start.10 = (f32[256,1024]{1,0:T(8,128)S(1)}, f32[256,1024]{1,0:T(8,128)}, u32[]{:S(2)}) copy-start(f32[256,1024]{1,0:T(8,128)} %copy-done.9) | copy-start | bytes 3145732
  837.4 70.6 %copy-start.51 = (f32[256]{0:T(256)S(1)}, f32[256]{0:T(256)}, u32[]{:S(2)}) copy-start(f32[256]{0:T(256)} %get-tuple-element.47) | copy-start | bytes 3076
  (40 other events, 100.6 us)
Sparse Core Ops, SparseCore 0:
  9.7 206.0 all-gather.5
  230.5 34.5 all-gather.7
  266.8 198.6 all-gather.9
  467.0 216.6 all-gather.11
  748.2 33.1 reduce-scatter.4
  784.3 644.6 reduce-scatter.8
  1431.9 667.0 reduce-scatter.6
  2102.0 724.7 reduce-scatter.10
where the time goes:
time: 2850 us; the launch traced here: 2830 us
  waiting for transfers between devices  2460 us (86%)
  blocking collectives  136 us (5%)
  matrix products  106 us (4%)
  other arithmetic  57.6 us (2%)
  local copies, waits for them, and re-layouts  55.1 us (2%)
    reduce_scatter x1, waiting for transfers between devices, shards(): lax.psum_scatter(mlp_term, ('seq', 'dp'), scatter_dimension=0, tiled=True)  728 us
    reduce_scatter x1, waiting for transfers between devices, shards(): lax.psum_scatter(qkv_term, ('seq', 'dp'), scatter_dimension=1, tiled=True)  670 us
    reduce_scatter x1, waiting for transfers between devices, shards(): lax.psum_scatter(out_term, ('seq', 'dp'), scatter_dimension=0, tiled=True)  520 us
    all_gather x1, waiting for transfers between devices, shards(): lax.all_gather(mlp_weight, ('seq', 'dp'), axis=0, tiled=True)  212 us
    all_gather x1, waiting for transfers between devices, shards(): lax.all_gather(out_weight, ('seq', 'dp'), axis=0, tiled=True)  179 us
    all_gather x1, waiting for transfers between devices, shards(): lax.all_gather(qkv_weight, ('seq', 'dp'), axis=1, tiled=True)  134 us
    unnamed x2, blocking collectives  133 us
  transfers between devices with their start and end apart: 8, of which 7 were waited for; matrix products, arithmetic and copies ran while one was open for 5% of the time, Pallas kernels for 0%

commit v1 on v0

v1 whole, which is shorter than its diff:
```python
import functools
import jax, jax.numpy as jnp
from jax import lax
from jax.experimental import pallas as pl
from jax.experimental.pallas import tpu as pltpu
from jax.sharding import PartitionSpec as P

MESH = pl.DeviceIdType.MESH
BF = jnp.bfloat16
F32 = jnp.float32
LQ = 256
HEAD = 128
EPSILON = 1e-06
THETA_BASE = 1000000.0
MASKED = -1e30
VMEM_BYTES = 63 << 20
SHAPES = {"q": (4, 2, 2, 2, 32, 1024), "k": (4, 2, 2, 2, 32, 1024), "o": (2, 2, 4, 2, 2, 16, 1024),
          "g": (4, 4, 2, 48, 1024), "u": (4, 4, 2, 48, 1024), "d": (4, 4, 2, 48, 1024)}
ORDERS = {"q": "xyz", "k": "yzx", "o": "zxy", "g": "xyz", "u": "yzx", "d": "zxy"}
KINDS = "qkogud"


def pick(kind, x, y, z, h):
    every = slice(None)
    at = lambda v: every if v is None else v
    low = lambda v: every if v is None else v % 2
    high = lambda v: every if v is None else v // 2
    lanes = every if z is None else pl.ds(pl.multiple_of(z * LQ, LQ), LQ)
    if kind == "q":
        return (at(y), low(x), at(h), high(x), every, lanes)
    if kind == "k":
        return (at(y), high(x), at(h), low(x), every, lanes)
    if kind == "o":
        return (at(h), high(y), at(x), every, low(y), every, lanes)
    return (at(x), at(y), at(h), every, lanes)


def half_shape(kind, full, axis):
    n = lambda a: 4 if a in full else None
    x, y, z = n("x"), n("y"), n("z")
    lanes = 1024 if z else 256
    if kind in "qk":
        s = ([4] if y else []) + ([2, 2] if x else []) + [32, lanes]
    elif kind == "o":
        s = ([2] if y else []) + ([4] if x else []) + [2] + ([2] if y else []) + [16, lanes]
    else:
        s = ([4] if x else []) + ([4] if y else []) + [48, lanes]
    return tuple(s)


class Place:
    def __init__(self):
        s, d = lax.axis_index("seq"), lax.axis_index("dp")
        self.zlo = s
        self.core = d % 2
        self.zhi = (d // 2) % 2
        self.x = (d // 4) % 4
        self.y = d // 16
        self.z = self.zhi * 2 + s

    def dev(self, x=None, y=None, z=None, core=None):
        x = self.x if x is None else x
        y = self.y if y is None else y
        z = self.z if z is None else z
        core = self.core if core is None else core
        return (z % 2, ((y * 4 + x) * 2 + z // 2) * 2 + core)

    def at(self, axis):
        return {"x": self.x, "y": self.y, "z": self.z}[axis]

    def ring(self, axis, step):
        return self.dev(**{axis: (self.at(axis) + step) % 4})


def flip(v):
    return v + 1 - 2 * (v % 2)


def region(me, kind, full, axis, val, h=None):
    c = {a: (None if a in full else me.at(a)) for a in "xyz"}
    c[axis] = val
    return pick(kind, c["x"], c["y"], c["z"], h)


def remote(src, dst, send, recv, device):
    return pltpu.make_async_remote_copy(src_ref=src, dst_ref=dst, send_sem=send, recv_sem=recv, device_id=device, device_id_type=MESH)


class Gather:
    def __init__(self, me, kind, phase, buf, send, recv, base):
        self.me, self.kind, self.buf, self.send, self.recv, self.base = me, kind, buf, send, recv, base
        order = ORDERS[kind]
        self.axis, self.full = order[phase], order[:phase]

    def reg(self, step, h=None):
        return self.buf.at[region(self.me, self.kind, self.full, self.axis, (self.me.at(self.axis) + step + 4) % 4, h)]

    def copy(self, n, step, h, hop):
        r = self.reg(step, h)
        return remote(r, r, self.send.at[self.base + n], self.recv.at[self.base + n], self.me.ring(self.axis, hop % 4))

    def start(self):
        self.copy(0, 0, None, 1).start()
        self.copy(1, 0, None, -1).start()

    def forward(self):
        self.copy(0, -1, None, 1).wait_recv()
        self.copy(2, -1, 0, 1).start()
        self.copy(1, 1, None, -1).wait_recv()
        self.copy(3, 1, 1, -1).start()

    def finish(self):
        self.copy(2, -2, 0, 1).wait_recv()
        self.copy(3, 2, 1, -1).wait_recv()

    def drain(self):
        self.copy(0, 0, None, 1).wait_send()
        self.copy(1, 0, None, -1).wait_send()
        self.copy(2, -1, 0, 1).wait_send()
        self.copy(3, 1, 1, -1).wait_send()


class Scatter:
    def __init__(self, me, kind, phase, buf, land, send, recv, base, final=None):
        self.me, self.kind, self.buf, self.land, self.send, self.recv, self.base = me, kind, buf, land, send, recv, base
        order = ORDERS[kind]
        self.axis, self.full = order[phase], order[:phase]
        self.final = final

    def idx(self, step, h):
        return region(self.me, self.kind, self.full, self.axis, (self.me.at(self.axis) + step + 4) % 4, h)

    def copy(self, n, src, hop):
        return remote(src, self.land.at[n], self.send.at[self.base + n], self.recv.at[self.base + n], self.me.ring(self.axis, hop % 4))

    def raw(self, n):
        step, h, hop = {4: (2, 0, 1), 5: (2, 1, -1), 1: (1, 1, 1), 3: (-1, 0, -1)}[n]
        return self.copy(n, self.buf.at[self.idx(step, h)], hop)

    def start(self):
        for n in (4, 5, 1, 3):
            self.raw(n).start()

    def forward(self):
        for n, step, h, to, hop in ((4, 1, 0, 0, 1), (5, -1, 1, 2, -1)):
            self.raw(n).wait_recv()
            total = self.land[n].astype(F32) + self.buf[self.idx(step, h)].astype(F32)
            self.land[n] = total.astype(BF)
            self.copy(to, self.land.at[n], hop).start()

    def finish(self):
        self.copy(0, self.land.at[4], 1).wait_recv()
        self.raw(3).wait_recv()
        self.raw(1).wait_recv()
        self.copy(2, self.land.at[5], -1).wait_recv()
        for h, a, b in ((0, 0, 3), (1, 2, 1)):
            total = self.land[a].astype(F32) + self.land[b].astype(F32) + self.buf[self.idx(0, h)].astype(F32)
            if self.final is None:
                self.buf[self.idx(0, h)] = total.astype(BF)
            else:
                self.final[h] = total

    def drain(self):
        for n in (4, 5, 1, 3):
            self.raw(n).wait_send()
        self.copy(0, self.land.at[4], 1).wait_send()
        self.copy(2, self.land.at[5], -1).wait_send()


def greet(me):
    bar = pltpu.get_barrier_semaphore()
    x, y, z, c = me.x, me.y, me.z, me.core
    friends = [me.ring("x", s) for s in (1, 2, 3)] + [me.ring("y", s) for s in (1, 2, 3)] + [me.ring("z", s) for s in (1, 2, 3)]
    friends.append(me.dev(core=1 - c))
    for s in range(4):
        zz = (z + s) % 4
        friends.append(me.dev(x=(x + 2) % 4, z=zz, core=1 - c))
        friends.append(me.dev(x=flip(x), z=zz, core=1 - c))
        friends.append(me.dev(y=flip(y), z=zz, core=1 - c))
    friends.append(me.dev(z=flip(z), core=1 - c))
    for f in friends:
        pl.semaphore_signal(bar, inc=1, device_id=f, device_id_type=MESH)
    pl.semaphore_wait(bar, len(friends))


class Route:
    def __init__(self, own, src, dst, send, recv, local, device):
        self.own = own
        self.made_far = lambda: remote(src, dst, send, recv, device)
        self.made_near = lambda: pltpu.make_async_copy(src, dst, local)

    def start(self):
        if self.own is None:
            self.made_far().start()
        else:
            pl.when(self.own)(lambda: self.made_near().start())
            pl.when(jnp.logical_not(self.own))(lambda: self.made_far().start())

    def wait_recv(self):
        if self.own is None:
            self.made_far().wait_recv()
        else:
            pl.when(self.own)(lambda: self.made_near().wait())
            pl.when(jnp.logical_not(self.own))(lambda: self.made_far().wait_recv())

    def wait_send(self):
        if self.own is None:
            self.made_far().wait_send()
        else:
            pl.when(jnp.logical_not(self.own))(lambda: self.made_far().wait_send())


def mapping(me, kind):
    x, y, c = me.x, me.y, me.core
    if kind == "q":
        own = (c + x // 2 + 1) % 2
        return own, dict(x=(x + 2 * (1 - own)) % 4, y=y, core=(c + 1 - own) % 2)
    if kind == "k":
        own = (c + x + 1) % 2
        return own, dict(x=x + (1 - own) * (1 - 2 * (x % 2)), y=y, core=(c + 1 - own) % 2)
    own = (c + y + 1) % 2
    return own, dict(x=x, y=y + (1 - own) * (1 - 2 * (y % 2)), core=(c + 1 - own) % 2)


def lanes_of(z):
    return pl.ds(pl.multiple_of(z * LQ, LQ), LQ)


class Spread:
    def __init__(self, me, wq, wo, wm, bufs, stage, send, recv, local):
        self.me, self.wq, self.wo, self.wm, self.bufs, self.stage = me, wq, wo, wm, bufs, stage
        self.send, self.recv, self.local = send, recv, local

    def qk(self, kind, dz, zsrc, to=None):
        me = self.me
        own, col = mapping(me, kind)
        z = (me.z + dz) % 4
        place = dict(x=me.x, y=me.y) if to is None else col
        dst = self.bufs[kind].at[pick_piece(kind, place["x"], place["y"], z, zsrc)]
        n = zsrc // 2
        return Route((own == 1) & (zsrc == z), self.wq.at[:, lanes_of(z)], dst, self.send.at[dz],
                     self.recv.at[(0 if kind == "q" else 2) + n], self.local.at[0], me.dev(z=z, **col))

    def o(self, dz, zsrc, place):
        me = self.me
        own, col = mapping(me, "o")
        z = (me.z + dz) % 4
        y = me.y if place is None else col["y"]
        dst = self.bufs["o"].at[zsrc % 2, y // 2, me.x, zsrc // 2, y % 2, slice(None), lanes_of(z)]
        return Route((own == 1) & (zsrc == z), self.wo.at[:, lanes_of(z)], dst, self.send.at[4 + dz],
                     self.recv.at[4 + zsrc], self.local.at[1], me.dev(z=z, **col))

    def m(self, dz):
        me = self.me
        z = (me.z + dz) % 4
        return remote(self.wm.at[:, lanes_of(z)], self.stage.at[dz], self.send.at[8 + dz], self.recv.at[8 + dz], me.dev(z=z))

    def start_attention(self):
        me = self.me
        for kind, low in (("q", 0), ("k", 1)):
            @pl.when(me.zlo == low)
            def _(kind=kind):
                for dz in range(4):
                    self.qk(kind, dz, me.z, to=1).start()
        for dz in range(4):
            self.o(dz, me.z, 1).start()

    def start_mlp(self):
        for dz in range(1, 4):
            self.m(dz).start()

    def wait_attention(self):
        for n in range(2):
            self.qk("q", 0, 2 * n).wait_recv()
            self.qk("k", 0, 2 * n + 1).wait_recv()
        for zs in range(4):
            self.o(0, zs, None).wait_recv()

    def wait_mlp(self):
        me = self.me
        for dz in range(1, 4):
            self.m(dz).wait_recv()
        self.stage[0] = self.wm[:, lanes_of(me.z)]
        for t, kind in enumerate("gud"):
            rows = [self.stage[(me.z - zs + 4) % 4, t * 24:(t + 1) * 24, :] for zs in range(4)]
            block = jnp.concatenate(rows, axis=0).astype(BF)
            for h in range(2):
                self.bufs[kind][me.x, me.y, h, :, lanes_of(me.z)] = block[h * 48:(h + 1) * 48]

    def drain(self):
        me = self.me
        for kind, low in (("q", 0), ("k", 1)):
            @pl.when(me.zlo == low)
            def _(kind=kind):
                for dz in range(4):
                    self.qk(kind, dz, me.z, to=1).wait_send()
        for dz in range(4):
            self.o(dz, me.z, 1).wait_send()
        for dz in range(1, 4):
            self.m(dz).wait_send()


def pick_piece(kind, x, y, z, zsrc):
    every = slice(None)
    if kind == "q":
        return (y, x % 2, zsrc // 2, x // 2, every, lanes_of(z))
    return (y, x // 2, zsrc // 2, x % 2, every, lanes_of(z))


class Collect:
    def __init__(self, me, oq, oo, om, finals, send, recv, local):
        self.me, self.oq, self.oo, self.om, self.finals = me, oq, oo, om, finals
        self.send, self.recv, self.local = send, recv, local

    def qk(self, kind, dz):
        me = self.me
        own, col = mapping(me, kind)
        z = (me.z + dz) % 4
        keep = (own == 1) if dz == 0 else None
        return Route(keep, self.finals[kind].at[z // 2], self.oq.at[:, lanes_of(me.z)], self.send.at[dz],
                     self.recv.at[dz], self.local.at[0], me.dev(z=z, **col))

    def o(self, dz):
        me = self.me
        own, col = mapping(me, "o")
        z = (me.z + dz) % 4
        keep = (own == 1) if dz == 0 else None
        return Route(keep, self.finals["o"].at[z % 2, z // 2], self.oo.at[:, lanes_of(me.z)], self.send.at[4 + dz],
                     self.recv.at[4 + dz], self.local.at[1], me.dev(z=z, **col))

    def m(self, t, kind, dz):
        me = self.me
        z = (me.z + dz) % 4
        n = 8 + 4 * t + dz
        src = self.finals[kind].at[z // 2, pl.ds(pl.multiple_of((z % 2) * 24, 8), 24)]
        dst = self.om.at[pl.ds(t * 24, 24), lanes_of(me.z)]
        if dz == 0:
            return pltpu.make_async_copy(src, dst, self.local.at[2 + t])
        return remote(src, dst, self.send.at[n], self.recv.at[n], me.dev(z=z))

    def each_qk(self, act):
        me = self.me
        for dz in range(4):
            for kind, low in (("q", 0), ("k", 1)):
                @pl.when((me.z + dz) % 2 == low)
                def _(kind=kind, dz=dz):
                    act(self.qk(kind, dz))

    def start(self, kind):
        if kind == "qk":
            self.each_qk(lambda r: r.start())
        elif kind == "o":
            for dz in range(4):
                self.o(dz).start()
        else:
            for dz in range(4):
                self.m("gud".index(kind), kind, dz).start()

    def finish(self, kind):
        me = self.me
        if kind == "qk":
            for dz in range(4):
                for k, low in (("q", 0), ("k", 1)):
                    @pl.when(me.zlo == low)
                    def _(k=k, dz=dz):
                        self.qk(k, dz).wait_recv()
            self.each_qk(lambda r: r.wait_send())
        elif kind == "o":
            for dz in range(4):
                self.o(dz).wait_recv()
                self.o(dz).wait_send()
        else:
            for dz in range(4):
                c = self.m("gud".index(kind), kind, dz)
                if dz == 0:
                    c.wait()
                else:
                    c.wait_recv()
                    c.wait_send()


def dot(a, b):
    return jnp.dot(a, b, preferred_element_type=F32)


def dot_t(a, b):
    return lax.dot_general(a, b, (((1,), (1,)), ((), ())), preferred_element_type=F32)


def dot_c(a, b):
    return lax.dot_general(a, b, (((0,), (0,)), ((), ())), preferred_element_type=F32)


def mean_last(v):
    return jnp.mean(v, axis=-1, keepdims=True)


def norm_scale(v):
    return lax.rsqrt(mean_last(v * v) + EPSILON)


def norm_back(dz, v, gain):
    r = norm_scale(v)
    n = v * r
    w = dz * gain
    return r * (w - n * mean_last(w * n)), dz * n


def fold_rows(v):
    return jnp.sum(v.reshape(v.shape[0] // 8, 8, v.shape[1]), axis=0)


def rows_of(i, n):
    return pl.ds(pl.multiple_of(i * n, n), n)


class SmallSum:
    def __init__(self, me, buf, land, send, recv):
        self.me, self.buf, self.land, self.send, self.recv = me, buf, land, send, recv

    def copies(self, stage):
        if stage == 0:
            return [remote(self.buf, self.land.at[0], self.send.at[0], self.recv.at[0], self.me.dev(core=1 - self.me.core))]
        first = 1 + 3 * (stage - 1)
        return [remote(self.buf, self.land.at[first + s], self.send.at[first + s], self.recv.at[first + s],
                       self.me.ring("xyz"[stage - 1], s + 1)) for s in range(3)]

    def start(self, stage):
        for c in self.copies(stage):
            c.start()

    def finish(self, stage):
        for c in self.copies(stage):
            c.wait()
        if stage == 0:
            self.buf[...] = self.buf[...] + self.land[0]
        else:
            first = 1 + 3 * (stage - 1)
            self.buf[...] = self.buf[...] + (self.land[first] + self.land[first + 1] + self.land[first + 2])


class Layer:
    def __init__(self, me, S):
        self.me = me
        self.__dict__.update(S)
        c = me.core
        self.mine = rows_of(c, 256)
        self.theirs = rows_of(1 - c, 256)
        self.peer = me.dev(core=1 - c)
        self.wq2 = self.bq.reshape(1024, 1024)
        self.wk2 = self.bk.reshape(1024, 1024)
        self.wo2 = self.bo.reshape(1024, 1024)
        self.wg2 = self.bg.reshape(1536, 1024)
        self.wu2 = self.bu.reshape(1536, 1024)
        self.wd2 = self.bd.reshape(1536, 1024)
        self.dq2 = self.tq.reshape(1024, 1024)
        self.dk2 = self.tk.reshape(1024, 1024)
        self.cx, self.mi = self.dq2.at[pl.ds(0, 512)], self.dq2.at[pl.ds(512, 512)]
        self.es = self.dp.at[:, pl.ds(0, 1024)]
        self.lob, self.igb = self.ct.at[pl.ds(0, 256)], self.ct.at[pl.ds(256, 256)]
        self.da, self.dc = self.dk2.at[pl.ds(0, 512)], self.dk2.at[pl.ds(512, 512)]

    def swap(self, n, src, dst):
        me = self.me
        return Route(me.core == me.zlo, src, dst, self.xsend.at[n], self.xrecv.at[n], self.xlocal.at[n],
                     me.dev(z=me.zhi * 2 + me.core, core=me.zlo))

    def share(self, n, src, dst):
        return remote(src, dst, self.xsend.at[n], self.xrecv.at[n], self.peer)

    def tokens_in(self):
        theirs_there = rows_of(self.me.zlo, 256)
        return [self.swap(0, self.x_in, self.xa.at[theirs_there]),
                self.swap(1, self.meta_in, self.meta.at[self.me.zlo]),
                self.swap(2, self.ct_in, self.ct.at[theirs_there])]

    def tokens_across(self):
        m = self.mine
        return [self.share(3, self.xa.at[m], self.xa.at[m]),
                self.share(4, self.meta.at[self.me.core], self.meta.at[self.me.core]),
                self.share(5, self.ct.at[m], self.ct.at[m])]

    def gains_rows(self):
        for i in range(8):
            cols = slice(i * 128, (i + 1) * 128)
            self.gv[0:1, cols] = self.ga[i:i + 1, :]
            self.gv[1:2, cols] = self.ga[8 + i:9 + i, :]
        self.gv[2:3, 0:128] = self.ga[16:17, :]
        self.gv[2:3, 128:256] = self.ga[17:18, :]

    def tables(self):
        for h in range(2):
            place = jnp.broadcast_to(self.meta[h, 1:2, :].astype(F32), (128, 256)).T
            angle = place * self.consts[0:1, :]
            self.cosine[h * 256:(h + 1) * 256] = jnp.cos(angle)
            self.sine[h * 256:(h + 1) * 256] = jnp.sin(angle) * self.consts[1:2, :]
        for q in range(2):
            seg_q = jnp.broadcast_to(self.meta[q, 0:1, :].astype(F32), (128, 256)).T[:, 0:1]
            for k in range(2):
                seg_k = self.meta[k, 0:1, :].astype(F32)
                row = lax.broadcasted_iota(jnp.int32, (256, 256), 0) + q * 256
                col = lax.broadcasted_iota(jnp.int32, (256, 256), 1) + k * 256
                allowed = (seg_q == seg_k) & (col <= row)
                self.mask[q * 256:(q + 1) * 256, k * 256:(k + 1) * 256] = jnp.where(allowed, 0.0, MASKED).astype(BF)

    def norm_in(self):
        gain = self.gv[0:1, :]

        @pl.loop(0, 8)
        def _(i):
            r = rows_of(i, 64)
            v = self.xa[r].astype(F32)
            self.xn[r] = (v * norm_scale(v) * gain).astype(BF)

    def rope(self, n):
        return n * self.cosine[...] + pltpu.roll(n, 64, 1) * self.sine[...]

    def unrope(self, d, rows):
        return d * self.cosine[rows] - pltpu.roll(d, 64, 1) * self.sine[rows]

    def project(self):
        gq, gk = self.gv[2:3, 0:128], self.gv[2:3, 128:256]

        @pl.loop(0, 4)
        def _(i):
            pre = dot_t(self.xn[...], self.wq2[rows_of(i, 256)])
            for g in range(2):
                v = pre[:, g * 128:(g + 1) * 128]
                cols = pl.ds(pl.multiple_of(i * 256 + g * 128, 128), 128)
                self.qp[:, cols] = v.astype(BF)
                self.qr[:, cols] = self.rope(v * norm_scale(v) * gq).astype(BF)

        @pl.loop(0, 2)
        def _(i):
            pre = dot_t(self.xn[...], self.wk2[rows_of(i, 256)])
            for g in range(2):
                v = pre[:, g * 128:(g + 1) * 128]
                cols = pl.ds(pl.multiple_of(i * 256 + g * 128, 128), 128)
                self.kp[:, cols] = v.astype(BF)
                self.kr[:, cols] = self.rope(v * norm_scale(v) * gk).astype(BF)
            self.vl[:, rows_of(i, 256)] = dot_t(self.xn[...], self.wk2[rows_of(i + 2, 256)]).astype(BF)

    def attend(self):
        factor = HEAD ** -0.5 * 1.4426950408889634

        @pl.loop(0, 4)
        def _(k):
            kcols = rows_of(k, 128)
            for b in range(2):
                n = 256 * (b + 1)
                rows = slice(b * 256, (b + 1) * 256)
                keys, values = self.kr[0:n, kcols], self.vl[0:n, kcols]
                for g in range(2):
                    qcols = pl.ds(pl.multiple_of(k * 256 + g * 128, 128), 128)
                    s = dot_t(self.qr[rows, qcols], keys)
                    p = jnp.exp2(s * factor + self.mask[rows, 0:n].astype(F32))
                    p = (p * (1.0 / jnp.sum(p, axis=-1, keepdims=True))).astype(BF)
                    (self.p0 if b == 0 else self.p1)[2 * k + g] = p
                    self.cx[rows, qcols] = dot(p, values).astype(BF)

    def exchange(self, n, chunk, land):
        cols = slice(chunk * 256, (chunk + 1) * 256)
        return self.share(n + chunk, self.es.at[:, cols], land.at[:, cols])

    def out_project(self):
        for j in range(4):
            cols = slice(j * 256, (j + 1) * 256)
            part = dot(self.cx[...], self.wo2[:, cols])
            self.es[:, cols] = part.astype(BF)
            self.exchange(6, j, self.r0).start()
            self.hid[:, cols] = part + self.xa[:, cols].astype(F32)

    def norm_mid(self):
        for j in range(4):
            self.exchange(6, j, self.r0).wait()
        gain = self.gv[1:2, :]

        @pl.loop(0, 8)
        def _(i):
            r = rows_of(i, 64)
            v = self.hid[r] + self.r0[r].astype(F32)
            self.hid[r] = v
            self.mi[r] = (v * norm_scale(v) * gain).astype(BF)

    def feed_forward(self, c):
        r = rows_of(c, 256)
        gate = dot_t(self.mi[...], self.wg2[r])
        up = dot_t(self.mi[...], self.wu2[r])
        back = dot_t(self.ct[...], self.wd2[r])
        sig = jax.nn.sigmoid(gate)
        silu = gate * sig
        act = (silu * up).astype(BF)
        d_gate = (back * up * sig * (1.0 + gate * (1.0 - sig))).astype(BF)
        d_up = (back * silu).astype(BF)
        self.acc_o[...] += dot(act, self.wd2[r])
        self.acc_d[...] += dot(d_gate, self.wg2[r]) + dot(d_up, self.wu2[r])
        self.wd2[r] = dot_c(act, self.ct[...]).astype(BF)
        self.wg2[r] = dot_c(d_gate, self.mi[...]).astype(BF)
        self.wu2[r] = dot_c(d_up, self.mi[...]).astype(BF)

    def send_mid(self):
        self.es[...] = self.acc_d[...].astype(BF)
        for j in range(4):
            self.exchange(10, j, self.r1).start()

    def norm_mid_back(self):
        for j in range(4):
            self.exchange(10, j, self.r1).wait()
        gain = self.gv[1:2, :]

        def body(i, total):
            r = rows_of(i, 64)
            dz = self.acc_d[r] + self.r1[r].astype(F32)
            dv, term = norm_back(dz, self.hid[r], gain)
            d = self.ct[r].astype(F32) + dv
            self.acc_d[r] = d
            self.da[r] = d.astype(BF)
            return total + fold_rows(term) * (i // 4 == self.me.core).astype(F32)

        total = lax.fori_loop(0, 8, body, jnp.zeros((8, 1024), F32))
        self.gg[1:2, :] = jnp.sum(total, axis=0, keepdims=True)

    def finish_output(self):
        self.ls[...] = self.acc_o[self.theirs].astype(BF)
        self.share(14, self.ls, self.r0.at[pl.ds(0, 256)]).start()
        self.share(14, self.ls, self.r0.at[pl.ds(0, 256)]).wait()
        self.lob[...] = (self.acc_o[self.mine] + self.hid[self.mine] + self.r0[0:256].astype(F32)).astype(BF)
        self.swap(15, self.lob, self.lo).start()

    def out_back(self):
        for j in range(4):
            r = slice(j * 256, (j + 1) * 256)
            self.dc[:, r] = dot_t(self.da[...], self.wo2[r]).astype(BF)
        for j in range(4):
            r = slice(j * 256, (j + 1) * 256)
            self.wo2[r] = dot_c(self.cx[:, r], self.da[...]).astype(BF)

    def attend_back(self):
        scale = HEAD ** -0.5
        gq, gk = self.gv[2:3, 0:128], self.gv[2:3, 128:256]

        def body(k, totals):
            total_q, total_k = totals
            kcols = rows_of(k, 128)
            dk, dv = [0.0, 0.0], [0.0, 0.0]
            for b in range(2):
                n = 256 * (b + 1)
                rows = slice(b * 256, (b + 1) * 256)
                keys, values = self.kr[0:n, kcols], self.vl[0:n, kcols]
                for g in range(2):
                    qcols = pl.ds(pl.multiple_of(k * 256 + g * 128, 128), 128)
                    low = (self.p0 if b == 0 else self.p1)[2 * k + g]
                    dc = self.dc[rows, qcols]
                    p = low.astype(F32)
                    t = p * dot_t(dc, values)
                    ds = (t - p * jnp.sum(t, axis=-1, keepdims=True)).astype(BF)
                    dz = self.unrope(dot(ds, keys) * scale, rows)
                    dq, term = norm_back(dz, self.qp[rows, qcols].astype(F32), gq)
                    self.dp[rows, qcols] = dq.astype(BF)
                    total_q = total_q + fold_rows(term)
                    pk, pv = dot_c(ds, self.qr[rows, qcols]), dot_c(low, dc)
                    for j in range(b + 1):
                        part = slice(j * 256, (j + 1) * 256)
                        dk[j] = dk[j] + pk[part]
                        dv[j] = dv[j] + pv[part]
            for j in range(2):
                rows = slice(j * 256, (j + 1) * 256)
                dz = self.unrope(dk[j] * scale, rows)
                dkey, term = norm_back(dz, self.kp[rows, kcols].astype(F32), gk)
                self.dp[rows, pl.ds(pl.multiple_of(1024 + k * 128, 128), 128)] = dkey.astype(BF)
                self.dp[rows, pl.ds(pl.multiple_of(1536 + k * 128, 128), 128)] = dv[j].astype(BF)
                total_k = total_k + fold_rows(term)
            return total_q, total_k

        zero = jnp.zeros((8, 128), F32)
        total_q, total_k = lax.fori_loop(0, 4, body, (zero, zero))
        self.gg[2:3, 0:128] = jnp.sum(total_q, axis=0, keepdims=True)
        self.gg[2:3, 128:256] = jnp.sum(total_k, axis=0, keepdims=True)

    def project_back(self):
        for grad, first in ((self.dq2, 0), (self.dk2, 1024)):
            @pl.loop(0, 4)
            def _(j, grad=grad, first=first):
                cols = pl.ds(pl.multiple_of(first + j * 256, 256), 256)
                grad[rows_of(j, 256)] = dot_c(self.dp[:, cols], self.xn[...]).astype(BF)

    def d_normed(self, rows):
        return dot(self.dp[rows, 0:1024], self.wq2[...]) + dot(self.dp[rows, 1024:2048], self.wk2[...])

    def send_in(self):
        self.ls[...] = self.d_normed(self.theirs).astype(BF)
        self.share(16, self.ls, self.r0.at[pl.ds(256, 256)]).start()

    def finish_input(self):
        self.hid[0:256] = self.d_normed(self.mine)
        self.share(16, self.ls, self.r0.at[pl.ds(256, 256)]).wait()
        gain = self.gv[0:1, :]

        def body(i, total):
            r = rows_of(i, 64)
            at = pl.ds(pl.multiple_of(self.me.core * 256 + i * 64, 64), 64)
            over = pl.ds(pl.multiple_of(256 + i * 64, 64), 64)
            dz = self.hid[r] + self.r0[over].astype(F32)
            dv, term = norm_back(dz, self.xa[at].astype(F32), gain)
            self.igb[r] = (self.acc_d[at] + dv).astype(BF)
            return total + fold_rows(term)

        total = lax.fori_loop(0, 4, body, jnp.zeros((8, 1024), F32))
        self.gg[0:1, :] = jnp.sum(total, axis=0, keepdims=True)
        self.swap(17, self.igb, self.ig).start()

    def gains_flat(self):
        for i in range(8):
            cols = slice(i * 128, (i + 1) * 128)
            self.gs[i:i + 1, :] = self.gg[0:1, cols]
            self.gs[8 + i:9 + i, :] = self.gg[1:2, cols]
        self.gs[16:17, :] = self.gg[2:3, 0:128]
        self.gs[17:18, :] = self.gg[2:3, 128:256]
        self.gs[18:24, :] = jnp.zeros((6, 128), F32)


INPUTS = ("x_in", "ct_in", "meta_in", "wq_in", "wo_in", "wm_in", "gain_in", "consts")
OUTPUTS = ("lo", "ig", "oq", "oo", "om", "gs")
V, SEM = pltpu.VMEM, pltpu.SemaphoreType.DMA


def scratch():
    s = {"b" + k: V(SHAPES[k], BF) for k in KINDS}
    s.update(tq=V(SHAPES["q"], BF), tk=V(SHAPES["k"], BF))
    s.update(stage=V((4, 72, 256), F32))
    s.update(xa=V((512, 1024), BF), ct=V((512, 1024), BF), meta=V((2, 8, 256), jnp.int32), xn=V((512, 1024), BF))
    s.update(qp=V((512, 1024), BF), kp=V((512, 512), BF), qr=V((512, 1024), BF), kr=V((512, 512), BF), vl=V((512, 512), BF))
    s.update(cosine=V((512, 128), F32), sine=V((512, 128), F32), mask=V((512, 512), BF))
    s.update(p0=V((8, 256, 256), BF), p1=V((8, 256, 512), BF))
    s.update(hid=V((512, 1024), F32), acc_o=V((512, 1024), F32), acc_d=V((512, 1024), F32))
    s.update(r0=V((512, 1024), BF), r1=V((512, 1024), BF))
    s.update(ls=V((256, 1024), BF))
    s.update(dp=V((512, 2048), BF))
    s.update(ga=V((24, 128), F32), gv=V((8, 1024), F32), gg=V((8, 1024), F32), land_a=V((10, 24, 128), F32), land_b=V((10, 24, 128), F32))
    for k in KINDS:
        for p in range(3):
            s["land_%s%d" % (k, p)] = V((6,) + half_shape(k, ORDERS[k][:p], ORDERS[k][p]), BF)
        s["final_" + k] = V({"q": (2, 32, 256), "k": (2, 32, 256), "o": (2, 2, 16, 256)}.get(k, (2, 48, 256)), F32)
    for name, n in (("spread", 12), ("gather", 72), ("scatter", 108), ("collect", 20), ("small_a", 10), ("small_b", 10)):
        s[name + "_send"], s[name + "_recv"] = SEM((n,)), SEM((n,))
    s.update(spread_local=SEM((2,)), collect_local=SEM((5,)), xsend=SEM((18,)), xrecv=SEM((18,)), xlocal=SEM((18,)))
    return s


def kernel(*refs):
    shapes = scratch()
    S = dict(zip(INPUTS + OUTPUTS + tuple(shapes), refs))
    me = Place()
    greet(me)
    L = Layer(me, S)
    bufs = {k: S["b" + k] for k in KINDS}
    grads = dict(bufs, q=S["tq"], k=S["tk"])
    finals = {k: S["final_" + k] for k in KINDS}
    sp = Spread(me, S["wq_in"], S["wo_in"], S["wm_in"], bufs, S["stage"], S["spread_send"], S["spread_recv"], S["spread_local"])
    sp.start_attention()
    arrive = L.tokens_in()
    for c in arrive:
        c.start()
    sp.start_mlp()
    S["ga"][...] = S["gain_in"][...]
    ga = SmallSum(me, S["ga"], S["land_a"], S["small_a_send"], S["small_a_recv"])
    gb = SmallSum(me, S["gs"], S["land_b"], S["small_b_send"], S["small_b_recv"])
    G = {(k, p): Gather(me, k, p, bufs[k], S["gather_send"], S["gather_recv"], (KINDS.index(k) * 3 + p) * 4)
         for k in KINDS for p in range(3)}
    sp.wait_attention()

    def gather(rnd):
        for p in range(3):
            for act in ("start", "forward", "finish"):
                for k in rnd:
                    getattr(G[k, p], act)()

    gather("qko")
    sp.wait_mlp()
    gather("gud")
    for c in arrive:
        c.wait_recv()
    across = L.tokens_across()
    for c in across:
        c.start()
    for stage in range(4):
        ga.start(stage)
        ga.finish(stage)
    for c in across:
        c.wait()
    for c in arrive:
        c.wait_send()
    for k in KINDS:
        for p in range(3):
            G[k, p].drain()
    sp.drain()
    L.gains_rows()
    L.tables()
    L.norm_in()
    L.project()
    L.attend()
    L.out_project()
    L.norm_mid()
    L.acc_o[...] = jnp.zeros((512, 1024), F32)
    L.acc_d[...] = jnp.zeros((512, 1024), F32)
    pl.loop(0, 6)(L.feed_forward)
    L.send_mid()
    L.norm_mid_back()
    L.finish_output()
    L.out_back()
    L.attend_back()
    L.project_back()
    L.send_in()
    L.finish_input()
    L.gains_flat()
    C = Collect(me, S["oq"], S["oo"], S["om"], finals, S["collect_send"], S["collect_recv"], S["collect_local"])
    R = {(k, p): Scatter(me, k, p, grads[k], S["land_%s%d" % (k, p)], S["scatter_send"], S["scatter_recv"],
                         (KINDS.index(k) * 3 + p) * 6, finals[k] if p == 0 else None) for k in KINDS for p in range(3)}

    def scatter(rnd):
        for p in (2, 1, 0):
            for act in ("start", "forward", "finish", "drain"):
                for k in rnd:
                    getattr(R[k, p], act)()

    scatter("gud")
    for k in "gud":
        C.start(k)
    for stage in range(4):
        gb.start(stage)
        gb.finish(stage)
    scatter("qko")
    C.start("o")
    C.start("qk")
    for k in ("g", "u", "d", "o", "qk"):
        C.finish(k)
    for n, src, dst in ((15, L.lob, L.lo), (17, L.igb, L.ig)):
        c = L.swap(n, src, dst)
        c.wait_recv()
        c.wait_send()


def shards(layer_input, segments, positions, qkv_weight, out_weight, mlp_weight, gains, cotangent):
    place = lax.axis_index("seq") * 64 + lax.axis_index("dp")
    meta = jnp.concatenate([segments, positions, jnp.zeros((6, 256), jnp.int32)], axis=0)
    wm = jnp.transpose(mlp_weight, (1, 0, 2)).reshape(72, 1024).astype(F32)
    gain = lax.dynamic_update_slice(jnp.zeros((3072,), F32), gains.astype(F32), (place * 18,)).reshape(24, 128)
    freqs = THETA_BASE ** (-(jnp.arange(64, dtype=F32) * 2.0) / HEAD)
    sign = jnp.concatenate([-jnp.ones((64,), F32), jnp.ones((64,), F32)])
    consts = jnp.stack([jnp.concatenate([freqs, freqs]), sign] + [sign] * 6)
    vm = pl.BlockSpec(memory_space=pltpu.VMEM)
    shape = jax.ShapeDtypeStruct
    lo, ig, oq, oo, om, gs = pl.pallas_call(
        kernel,
        out_shape=(shape((256, 1024), BF), shape((256, 1024), BF), shape((32, 1024), F32), shape((16, 1024), F32),
                   shape((72, 1024), F32), shape((24, 128), F32)),
        in_specs=[vm] * len(INPUTS),
        out_specs=(vm,) * len(OUTPUTS),
        scratch_shapes=list(scratch().values()),
        compiler_params=pltpu.CompilerParams(collective_id=0, has_side_effects=True, vmem_limit_bytes=VMEM_BYTES),
    )(layer_input[0], cotangent[0], meta, qkv_weight.T, out_weight, wm, gain, consts)
    return (lo[None], ig[None], oq.T, oo, jnp.transpose(om.reshape(3, 24, 1024), (1, 0, 2)),
            lax.dynamic_slice(gs.reshape(3072), (place * 18,), (18,)))


def solution(mesh):
    rows, split = P("dp", "seq", None), ("seq", "dp")
    weights = (P(None, split), P(split, None), P(split, None, None), P(split))
    return jax.shard_map(shards, mesh=mesh, in_specs=(rows, P("dp", "seq"), P("dp", "seq")) + weights + (rows,),
                         out_specs=(rows, rows) + weights, check_vma=False)
```

time: 2850 us -> 299 us (0.10)
  waiting for transfers between devices: 2460 us -> 0 us
  Pallas kernels: 0 us -> 287 us
  blocking collectives: 136 us -> 0 us
  matrix products: 106 us -> 0 us
  other arithmetic: 57.6 us -> 2.49 us
  local copies, waits for them, and re-layouts: 55.1 us -> 8.24 us
    reduce_scatter x4 -> x0, waiting for transfers between devices: 1920 us -> none  [the longest x1 728 us: shards(): lax.psum_scatter(mlp_term, ('seq', 'dp'), scatter_dimension=0, tiled=True)]
    all_gather x4 -> x0, waiting for transfers between devices: 544 us -> none  [the longest x1 212 us: shards(): lax.all_gather(mlp_weight, ('seq', 'dp'), axis=0, tiled=True)]
    pallas_call x0 -> x1, Pallas kernels: none -> 287 us  [shards(): pl.pallas_call(kernel, out_shape=(shape((256, 1024), BF), shape((256, 102...]
    unnamed x2 -> x0, blocking collectives: 133 us -> none
    dot_general x20 -> x0, matrix products: 97.8 us -> none  [the longest x5 25 us: contract_last(): lax.dot_general(left, right, (((1,), (1,)), ((), ())), preferred_element_...]
  transfers between devices with their start and end apart: 8 -> 0, of which waited for: 7 -> 0; matrix products, arithmetic and copies ran while one was open for 5% -> 0% of each run, Pallas kernels for 0% -> 0%
where the time goes in v1:
time: 299 us
  Pallas kernels  287 us (96%)
  local copies, waits for them, and re-layouts  8.24 us (3%)
    pallas_call x1, Pallas kernels, shards(): pl.pallas_call(kernel, out_shape=(shape((256, 1024), BF), shape((256, 102...  287 us
    unnamed x23, local copies, waits for them, and re-layouts  6.26 us

profile of v1, /device:TPU:1, one launch (start us, length us, event | category | flops | bytes accessed | tf_op | source)
XLA Modules:
  0.0 298.6 jit_solution(15886804734495039804)
XLA Ops:
  0.6 0.1 pad.4.clone
  0.7 0.0 copy-start.5
  0.7 0.1 maximum_bitcast_fusion
  0.8 0.6 copy-done.5
  1.4 0.0 copy-start.6
  1.4 0.6 stack.7.refs_7_
  2.0 0.1 copy-done.6
  2.1 0.0 copy-done.7
  2.1 0.7 add_add_fusion.refs_2_
  2.8 0.7 copy-done.8
  3.4 0.1 convert_dynamic-update-slice_fusion
  3.5 1.7 convert_element_type.15
  5.2 0.0 copy-done.4
  5.2 287.2 %shard_map.127 = (bf16[256,1024]{1,0:T(8,128)(2,1)}, bf16[256,1024]{1,0:T(8,128)(2,1)}, f32[32,1024]{1,0:T(8,128)}, f32[16,1024]{1,0:T(8,128)}, f32[72,1024]{1,0:T(8,128)}, /*index=5*/f32[24,128]{1,0:T(8,128)}) custom-call(bf16[256,1024]{1,0:T(8,128)(2,1)} %bitcast.19, bf16[256,1024]{1,0:T(8,128)(2,1)} %bitcast.20, s32[8,256]{1,0:T(8,128)} %add_add_fusion.refs_2_, ...), custom_call_target="tpu_custom_call" | custom-call | tf_op jit(solution)/shard_map/pallas_call | solution.py:853
  292.3 1.3 dynamic_slice.3
  293.6 1.9 copy.20
  295.6 0.0 copy-done
  295.6 0.8 copy.21
  296.4 0.2 copy-done.2
  296.6 0.7 copy.22
  297.2 0.0 copy-done.3
  297.2 0.6 copy.23
  297.9 0.0 copy-done.1
  297.9 0.7 copy.24
  (10 shorter events, 0.0 us)
Async XLA Ops:
  0.7 0.7 copy-start.5
  1.4 0.7 copy-start.6
  1.4 0.7 copy-start.7
  2.8 0.7 copy-start.8
  3.5 1.7 copy-start.4
  293.6 1.9 copy-start
  295.6 1.0 copy-start.2
  295.6 1.7 copy-start.3
  296.6 1.3 copy-start.1

commit v2 on v1

--- a/solution.py
+++ b/solution.py
@@ -1,4 +1,4 @@
-import functools
+import math
 import jax, jax.numpy as jnp
 from jax import lax
 from jax.experimental import pallas as pl
@@ -15,12 +15,14 @@
 MASKED = -1e30
 VMEM_BYTES = 63 << 20
 SHAPES = {"q": (4, 2, 2, 2, 32, 1024), "k": (4, 2, 2, 2, 32, 1024), "o": (2, 2, 4, 2, 2, 16, 1024),
-          "g": (4, 4, 2, 48, 1024), "u": (4, 4, 2, 48, 1024), "d": (4, 4, 2, 48, 1024)}
+          **{k: (2, 4, 4, 48, 1024) for k in "gud"}}
 ORDERS = {"q": "xyz", "k": "yzx", "o": "zxy", "g": "xyz", "u": "yzx", "d": "zxy"}
 KINDS = "qkogud"
-
-
-def pick(kind, x, y, z, h):
+ATT, MLP = "qko", "gud"
+PHASES = {k: [(0, None), (1, None)] + ([(2, 0), (2, 1)] if k in "gud" else [(2, None)]) for k in KINDS}
+
+
+def pick(kind, x, y, z, h, chunk):
     every = slice(None)
     at = lambda v: every if v is None else v
     low = lambda v: every if v is None else v % 2
@@ -32,10 +34,12 @@
         return (at(y), high(x), at(h), low(x), every, lanes)
     if kind == "o":
         return (at(h), high(y), at(x), every, low(y), every, lanes)
-    return (at(x), at(y), at(h), every, lanes)
-
-
-def half_shape(kind, full, axis):
+    if h is not None:
+        lanes = pl.ds(h * 512, 512) if z is None else pl.ds(pl.multiple_of(z * LQ + h * 128, 128), 128)
+    return (at(chunk), at(x), at(y), every, lanes)
+
+
+def half_shape(kind, full, axis, chunk):
     n = lambda a: 4 if a in full else None
     x, y, z = n("x"), n("y"), n("z")
     lanes = 1024 if z else 256
@@ -44,14 +48,14 @@
     elif kind == "o":
         s = ([2] if y else []) + ([4] if x else []) + [2] + ([2] if y else []) + [16, lanes]
     else:
-        s = ([4] if x else []) + ([4] if y else []) + [48, lanes]
+        s = ([2] if chunk is None else []) + ([4] if x else []) + ([4] if y else []) + [48, lanes // 2]
     return tuple(s)
 
 
 class Place:
     def __init__(self):
         s, d = lax.axis_index("seq"), lax.axis_index("dp")
-        self.zlo = s
+        self.zlo, self.dp = s, d
         self.core = d % 2
         self.zhi = (d // 2) % 2
         self.x = (d // 4) % 4
@@ -76,95 +80,102 @@
     return v + 1 - 2 * (v % 2)
 
 
-def region(me, kind, full, axis, val, h=None):
+def block_rows(kind, phase, chunk):
+    return 4 ** phase * (16 if kind in ATT else 24 if chunk is None else 12)
+
+
+def ruler(ref, rows):
+    for lanes in (1024, 768, 512, 256):
+        n = rows * 1024 // lanes
+        if rows * 1024 % lanes == 0 and n % 16 == 0 and n <= ref.shape[0]:
+            return ref.at[pl.ds(0, n), pl.ds(0, lanes)]
+    raise ValueError(rows)
+
+
+def region(me, kind, full, axis, val, h=None, chunk=None):
     c = {a: (None if a in full else me.at(a)) for a in "xyz"}
     c[axis] = val
-    return pick(kind, c["x"], c["y"], c["z"], h)
+    return pick(kind, c["x"], c["y"], c["z"], h, chunk)
 
 
 def remote(src, dst, send, recv, device):
     return pltpu.make_async_remote_copy(src_ref=src, dst_ref=dst, send_sem=send, recv_sem=recv, device_id=device, device_id_type=MESH)
 
 
-class Gather:
-    def __init__(self, me, kind, phase, buf, send, recv, base):
-        self.me, self.kind, self.buf, self.send, self.recv, self.base = me, kind, buf, send, recv, base
+class Phase:
+    def __init__(self, me, kind, phase, chunk, buf, land, measure, send, recv, final=None):
+        self.me, self.kind, self.chunk, self.buf, self.land, self.measure = me, kind, chunk, buf, land, measure
+        self.send, self.recv, self.final = send, recv, final
         order = ORDERS[kind]
         self.axis, self.full = order[phase], order[:phase]
-
-    def reg(self, step, h=None):
-        return self.buf.at[region(self.me, self.kind, self.full, self.axis, (self.me.at(self.axis) + step + 4) % 4, h)]
-
-    def copy(self, n, step, h, hop):
-        r = self.reg(step, h)
-        return remote(r, r, self.send.at[self.base + n], self.recv.at[self.base + n], self.me.ring(self.axis, hop % 4))
+        self.rows = block_rows(kind, phase, chunk)
+        self.small = phase == 0
+
+    def idx(self, step, h=None):
+        return region(self.me, self.kind, self.full, self.axis, (self.me.at(self.axis) + step + 4) % 4, h, self.chunk)
+
+    def push(self, src, dst, n, hop):
+        remote(src, dst, self.send, self.recv[n], self.me.ring(self.axis, hop % 4)).start()
+
+    def take(self, n, regions):
+        r = ruler(self.measure, self.rows * regions)
+        remote(r, r, self.send, self.recv[n], self.me.ring(self.axis, 1)).wait_recv()
+
+
+class Gather(Phase):
+    def copy(self, step, h, n, hop):
+        r = self.buf.at[self.idx(step, h)]
+        self.push(r, r, n, hop)
 
     def start(self):
-        self.copy(0, 0, None, 1).start()
-        self.copy(1, 0, None, -1).start()
+        self.copy(0, None, 0, 1)
+        self.copy(0, None, 0, -1)
+        if self.small:
+            self.copy(0, None, 0, 2)
 
     def forward(self):
-        self.copy(0, -1, None, 1).wait_recv()
-        self.copy(2, -1, 0, 1).start()
-        self.copy(1, 1, None, -1).wait_recv()
-        self.copy(3, 1, 1, -1).start()
+        self.take(0, 2)
+        self.copy(-1, 0, 1, 1)
+        self.copy(1, 1, 1, -1)
 
     def finish(self):
-        self.copy(2, -2, 0, 1).wait_recv()
-        self.copy(3, 2, 1, -1).wait_recv()
-
-    def drain(self):
-        self.copy(0, 0, None, 1).wait_send()
-        self.copy(1, 0, None, -1).wait_send()
-        self.copy(2, -1, 0, 1).wait_send()
-        self.copy(3, 1, 1, -1).wait_send()
-
-
-class Scatter:
-    def __init__(self, me, kind, phase, buf, land, send, recv, base, final=None):
-        self.me, self.kind, self.buf, self.land, self.send, self.recv, self.base = me, kind, buf, land, send, recv, base
-        order = ORDERS[kind]
-        self.axis, self.full = order[phase], order[:phase]
-        self.final = final
-
-    def idx(self, step, h):
-        return region(self.me, self.kind, self.full, self.axis, (self.me.at(self.axis) + step + 4) % 4, h)
-
-    def copy(self, n, src, hop):
-        return remote(src, self.land.at[n], self.send.at[self.base + n], self.recv.at[self.base + n], self.me.ring(self.axis, hop % 4))
-
-    def raw(self, n):
-        step, h, hop = {4: (2, 0, 1), 5: (2, 1, -1), 1: (1, 1, 1), 3: (-1, 0, -1)}[n]
-        return self.copy(n, self.buf.at[self.idx(step, h)], hop)
+        self.take(0, 3) if self.small else self.take(1, 1)
+
+
+class Scatter(Phase):
+    def raw(self, to, step, h, n, hop):
+        self.push(self.buf.at[self.idx(step, h)], self.land.at[to], n, hop)
 
     def start(self):
-        for n in (4, 5, 1, 3):
-            self.raw(n).start()
+        if self.small:
+            for step in (1, 3, 2):
+                for h in range(2):
+                    self.raw(2 * (step - 1) + h, step, h, 1, step)
+            return
+        self.raw(4, 2, 0, 0, 1)
+        self.raw(5, 2, 1, 0, -1)
+        self.raw(1, 1, 1, 1, 1)
+        self.raw(3, -1, 0, 1, -1)
 
     def forward(self):
-        for n, step, h, to, hop in ((4, 1, 0, 0, 1), (5, -1, 1, 2, -1)):
-            self.raw(n).wait_recv()
-            total = self.land[n].astype(F32) + self.buf[self.idx(step, h)].astype(F32)
-            self.land[n] = total.astype(BF)
-            self.copy(to, self.land.at[n], hop).start()
+        self.take(0, 1)
+        for at, step, h, to, hop in ((4, 1, 0, 0, 1), (5, -1, 1, 2, -1)):
+            total = self.land[at].astype(F32) + self.buf[self.idx(step, h)].astype(F32)
+            self.land[at] = total.astype(BF)
+            self.push(self.land.at[at], self.land.at[to], 1, hop)
 
     def finish(self):
-        self.copy(0, self.land.at[4], 1).wait_recv()
-        self.raw(3).wait_recv()
-        self.raw(1).wait_recv()
-        self.copy(2, self.land.at[5], -1).wait_recv()
-        for h, a, b in ((0, 0, 3), (1, 2, 1)):
-            total = self.land[a].astype(F32) + self.land[b].astype(F32) + self.buf[self.idx(0, h)].astype(F32)
+        self.take(1, 3 if self.small else 2)
+        for h, slots in ((0, (0, 2, 4) if self.small else (0, 3)), (1, (1, 3, 5) if self.small else (2, 1))):
+            total = self.buf[self.idx(0, h)].astype(F32)
+            for a in slots:
+                total = total + self.land[a].astype(F32)
             if self.final is None:
                 self.buf[self.idx(0, h)] = total.astype(BF)
+            elif self.kind in MLP:
+                self.final[:, :, h * 128:(h + 1) * 128] = total
             else:
                 self.final[h] = total
-
-    def drain(self):
-        for n in (4, 5, 1, 3):
-            self.raw(n).wait_send()
-        self.copy(0, self.land.at[4], 1).wait_send()
-        self.copy(2, self.land.at[5], -1).wait_send()
 
 
 def greet(me):
@@ -284,8 +295,8 @@
         for t, kind in enumerate("gud"):
             rows = [self.stage[(me.z - zs + 4) % 4, t * 24:(t + 1) * 24, :] for zs in range(4)]
             block = jnp.concatenate(rows, axis=0).astype(BF)
-            for h in range(2):
-                self.bufs[kind][me.x, me.y, h, :, lanes_of(me.z)] = block[h * 48:(h + 1) * 48]
+            for j in range(2):
+                self.bufs[kind][j, me.x, me.y, :, lanes_of(me.z)] = block[j * 48:(j + 1) * 48]
 
     def drain(self):
         me = self.me
@@ -422,7 +433,7 @@
         if stage == 0:
             return [remote(self.buf, self.land.at[0], self.send.at[0], self.recv.at[0], self.me.dev(core=1 - self.me.core))]
         first = 1 + 3 * (stage - 1)
-        return [remote(self.buf, self.land.at[first + s], self.send.at[first + s], self.recv.at[first + s],
+        return [remote(self.buf, self.land.at[first + s], self.send.at[stage], self.recv.at[stage],
                        self.me.ring("xyz"[stage - 1], s + 1)) for s in range(3)]
 
     def start(self, stage):
@@ -430,12 +441,13 @@
             c.start()
 
     def finish(self, stage):
-        for c in self.copies(stage):
-            c.wait()
         if stage == 0:
+            self.copies(0)[0].wait()
             self.buf[...] = self.buf[...] + self.land[0]
         else:
             first = 1 + 3 * (stage - 1)
+            three = self.land.at[pl.ds(first, 3)]
+            remote(three, three, self.send.at[stage], self.recv.at[stage], self.me.ring("xyz"[stage - 1], 1)).wait()
             self.buf[...] = self.buf[...] + (self.land[first] + self.land[first + 1] + self.land[first + 2])
 
 
@@ -450,9 +462,7 @@
         self.wq2 = self.bq.reshape(1024, 1024)
         self.wk2 = self.bk.reshape(1024, 1024)
         self.wo2 = self.bo.reshape(1024, 1024)
-        self.wg2 = self.bg.reshape(1536, 1024)
-        self.wu2 = self.bu.reshape(1536, 1024)
-        self.wd2 = self.bd.reshape(1536, 1024)
+        self.mlp = [[S["b" + k].at[j].reshape(768, 1024) for k in "gud"] for j in range(2)]
         self.dq2 = self.tq.reshape(1024, 1024)
         self.dk2 = self.tk.reshape(1024, 1024)
         self.cx, self.mi = self.dq2.at[pl.ds(0, 512)], self.dq2.at[pl.ds(512, 512)]
@@ -469,16 +479,23 @@
         return remote(src, dst, self.xsend.at[n], self.xrecv.at[n], self.peer)
 
     def tokens_in(self):
-        theirs_there = rows_of(self.me.zlo, 256)
-        return [self.swap(0, self.x_in, self.xa.at[theirs_there]),
-                self.swap(1, self.meta_in, self.meta.at[self.me.zlo]),
-                self.swap(2, self.ct_in, self.ct.at[theirs_there])]
+        there = self.me.zlo
+        return [self.swap(0, self.x_in, self.xa.at[rows_of(there, 256)]),
+                self.swap(1, self.seg_in, self.seg.at[there]),
+                self.swap(2, self.pos_in, self.pos.at[there]),
+                self.swap(3, self.ct_in, self.ct.at[rows_of(there, 256)])]
+
+    def send_piece(self, n, i):
+        src, dst = (self.x_in, self.xa) if n == 0 else (self.ct_in, self.ct)
+        self.swap(n, src.at[pl.ds(i * 64, 64)], dst.at[pl.ds(pl.multiple_of(self.me.zlo * 256 + i * 64, 64), 64)]).start()
 
     def tokens_across(self):
         m = self.mine
-        return [self.share(3, self.xa.at[m], self.xa.at[m]),
-                self.share(4, self.meta.at[self.me.core], self.meta.at[self.me.core]),
-                self.share(5, self.ct.at[m], self.ct.at[m])]
+        c = self.me.core
+        return [self.share(4, self.xa.at[m], self.xa.at[m]),
+                self.share(5, self.seg.at[c], self.seg.at[c]),
+                self.share(6, self.pos.at[c], self.pos.at[c]),
+                self.share(7, self.ct.at[m], self.ct.at[m])]
 
     def gains_rows(self):
         for i in range(8):
@@ -489,15 +506,17 @@
         self.gv[2:3, 128:256] = self.ga[17:18, :]
 
     def tables(self):
+        lane = lax.broadcasted_iota(jnp.int32, (1, 128), 1)
+        freqs = jnp.exp((lane % 64).astype(F32) * (-2.0 * math.log(THETA_BASE) / HEAD))
+        sign = jnp.where(lane < 64, -1.0, 1.0)
         for h in range(2):
-            place = jnp.broadcast_to(self.meta[h, 1:2, :].astype(F32), (128, 256)).T
-            angle = place * self.consts[0:1, :]
+            angle = jnp.broadcast_to(self.pos[h].astype(F32), (128, 256)).T * freqs
             self.cosine[h * 256:(h + 1) * 256] = jnp.cos(angle)
-            self.sine[h * 256:(h + 1) * 256] = jnp.sin(angle) * self.consts[1:2, :]
+            self.sine[h * 256:(h + 1) * 256] = jnp.sin(angle) * sign
         for q in range(2):
-            seg_q = jnp.broadcast_to(self.meta[q, 0:1, :].astype(F32), (128, 256)).T[:, 0:1]
+            seg_q = jnp.broadcast_to(self.seg[q].astype(F32), (128, 256)).T[:, 0:1]
             for k in range(2):
-                seg_k = self.meta[k, 0:1, :].astype(F32)
+                seg_k = self.seg[k].astype(F32)
                 row = lax.broadcasted_iota(jnp.int32, (256, 256), 0) + q * 256
                 col = lax.broadcasted_iota(jnp.int32, (256, 256), 1) + k * 256
                 allowed = (seg_q == seg_k) & (col <= row)
@@ -567,12 +586,12 @@
             cols = slice(j * 256, (j + 1) * 256)
             part = dot(self.cx[...], self.wo2[:, cols])
             self.es[:, cols] = part.astype(BF)
-            self.exchange(6, j, self.r0).start()
+            self.exchange(8, j, self.r0).start()
             self.hid[:, cols] = part + self.xa[:, cols].astype(F32)
 
     def norm_mid(self):
         for j in range(4):
-            self.exchange(6, j, self.r0).wait()
+            self.exchange(8, j, self.r0).wait()
         gain = self.gv[1:2, :]
 
         @pl.loop(0, 8)
@@ -582,30 +601,31 @@
             self.hid[r] = v
             self.mi[r] = (v * norm_scale(v) * gain).astype(BF)
 
-    def feed_forward(self, c):
+    def feed_forward(self, j, c):
+        wg2, wu2, wd2 = self.mlp[j]
         r = rows_of(c, 256)
-        gate = dot_t(self.mi[...], self.wg2[r])
-        up = dot_t(self.mi[...], self.wu2[r])
-        back = dot_t(self.ct[...], self.wd2[r])
+        gate = dot_t(self.mi[...], wg2[r])
+        up = dot_t(self.mi[...], wu2[r])
+        back = dot_t(self.ct[...], wd2[r])
         sig = jax.nn.sigmoid(gate)
         silu = gate * sig
         act = (silu * up).astype(BF)
         d_gate = (back * up * sig * (1.0 + gate * (1.0 - sig))).astype(BF)
         d_up = (back * silu).astype(BF)
-        self.acc_o[...] += dot(act, self.wd2[r])
-        self.acc_d[...] += dot(d_gate, self.wg2[r]) + dot(d_up, self.wu2[r])
-        self.wd2[r] = dot_c(act, self.ct[...]).astype(BF)
-        self.wg2[r] = dot_c(d_gate, self.mi[...]).astype(BF)
-        self.wu2[r] = dot_c(d_up, self.mi[...]).astype(BF)
+        self.acc_o[...] += dot(act, wd2[r])
+        self.acc_d[...] += dot(d_gate, wg2[r]) + dot(d_up, wu2[r])
+        wd2[r] = dot_c(act, self.ct[...]).astype(BF)
+        wg2[r] = dot_c(d_gate, self.mi[...]).astype(BF)
+        wu2[r] = dot_c(d_up, self.mi[...]).astype(BF)
 
     def send_mid(self):
         self.es[...] = self.acc_d[...].astype(BF)
         for j in range(4):
-            self.exchange(10, j, self.r1).start()
+            self.exchange(12, j, self.r1).start()
 
     def norm_mid_back(self):
         for j in range(4):
-            self.exchange(10, j, self.r1).wait()
+            self.exchange(12, j, self.r1).wait()
         gain = self.gv[1:2, :]
 
         def body(i, total):
@@ -622,10 +642,9 @@
 
     def finish_output(self):
         self.ls[...] = self.acc_o[self.theirs].astype(BF)
-        self.share(14, self.ls, self.r0.at[pl.ds(0, 256)]).start()
-        self.share(14, self.ls, self.r0.at[pl.ds(0, 256)]).wait()
+        self.share(16, self.ls, self.r0.at[pl.ds(0, 256)]).start()
+        self.share(16, self.ls, self.r0.at[pl.ds(0, 256)]).wait()
         self.lob[...] = (self.acc_o[self.mine] + self.hid[self.mine] + self.r0[0:256].astype(F32)).astype(BF)
-        self.swap(15, self.lob, self.lo).start()
 
     def out_back(self):
         for j in range(4):
@@ -635,7 +654,7 @@
             r = slice(j * 256, (j + 1) * 256)
             self.wo2[r] = dot_c(self.cx[:, r], self.da[...]).astype(BF)
 
-    def attend_back(self):
+    def attend_back(self, between):
         scale = HEAD ** -0.5
         gq, gk = self.gv[2:3, 0:128], self.gv[2:3, 128:256]
 
@@ -670,6 +689,7 @@
                 self.dp[rows, pl.ds(pl.multiple_of(1024 + k * 128, 128), 128)] = dkey.astype(BF)
                 self.dp[rows, pl.ds(pl.multiple_of(1536 + k * 128, 128), 128)] = dv[j].astype(BF)
                 total_k = total_k + fold_rows(term)
+            between(k)
             return total_q, total_k
 
         zero = jnp.zeros((8, 128), F32)
@@ -677,23 +697,24 @@
         self.gg[2:3, 0:128] = jnp.sum(total_q, axis=0, keepdims=True)
         self.gg[2:3, 128:256] = jnp.sum(total_k, axis=0, keepdims=True)
 
-    def project_back(self):
-        for grad, first in ((self.dq2, 0), (self.dk2, 1024)):
-            @pl.loop(0, 4)
-            def _(j, grad=grad, first=first):
-                cols = pl.ds(pl.multiple_of(first + j * 256, 256), 256)
-                grad[rows_of(j, 256)] = dot_c(self.dp[:, cols], self.xn[...]).astype(BF)
+    def project_back(self, kind):
+        grad, first = (self.dq2, 0) if kind == "q" else (self.dk2, 1024)
+
+        @pl.loop(0, 4)
+        def _(j):
+            cols = pl.ds(pl.multiple_of(first + j * 256, 256), 256)
+            grad[rows_of(j, 256)] = dot_c(self.dp[:, cols], self.xn[...]).astype(BF)
 
     def d_normed(self, rows):
         return dot(self.dp[rows, 0:1024], self.wq2[...]) + dot(self.dp[rows, 1024:2048], self.wk2[...])
 
     def send_in(self):
         self.ls[...] = self.d_normed(self.theirs).astype(BF)
-        self.share(16, self.ls, self.r0.at[pl.ds(256, 256)]).start()
+        self.share(18, self.ls, self.r0.at[pl.ds(256, 256)]).start()
 
     def finish_input(self):
         self.hid[0:256] = self.d_normed(self.mine)
-        self.share(16, self.ls, self.r0.at[pl.ds(256, 256)]).wait()
+        self.share(18, self.ls, self.r0.at[pl.ds(256, 256)]).wait()
         gain = self.gv[0:1, :]
 
         def body(i, total):
@@ -707,7 +728,6 @@
 
         total = lax.fori_loop(0, 4, body, jnp.zeros((8, 1024), F32))
         self.gg[0:1, :] = jnp.sum(total, axis=0, keepdims=True)
-        self.swap(17, self.igb, self.ig).start()
 
     def gains_flat(self):
         for i in range(8):
@@ -719,7 +739,7 @@
         self.gs[18:24, :] = jnp.zeros((6, 128), F32)
 
 
-INPUTS = ("x_in", "ct_in", "meta_in", "wq_in", "wo_in", "wm_in", "gain_in", "consts")
+INPUTS = ("x_in", "ct_in", "seg_in", "pos_in", "wq_in", "wo_in", "wm_in", "gain_in")
 OUTPUTS = ("lo", "ig", "oq", "oo", "om", "gs")
 V, SEM = pltpu.VMEM, pltpu.SemaphoreType.DMA
 
@@ -727,8 +747,8 @@
 def scratch():
     s = {"b" + k: V(SHAPES[k], BF) for k in KINDS}
     s.update(tq=V(SHAPES["q"], BF), tk=V(SHAPES["k"], BF))
-    s.update(stage=V((4, 72, 256), F32))
-    s.update(xa=V((512, 1024), BF), ct=V((512, 1024), BF), meta=V((2, 8, 256), jnp.int32), xn=V((512, 1024), BF))
+    s.update(stage=V((4, 72, 256), F32), wqt=V((32, 1024), BF), wov=V((16, 1024), BF), wmv=V((3, 24, 1024), BF), wmf=V((72, 1024), F32))
+    s.update(xa=V((512, 1024), BF), ct=V((512, 1024), BF), seg=V((2, 1, 256), jnp.int32), pos=V((2, 1, 256), jnp.int32), xn=V((512, 1024), BF))
     s.update(qp=V((512, 1024), BF), kp=V((512, 512), BF), qr=V((512, 1024), BF), kr=V((512, 512), BF), vl=V((512, 512), BF))
     s.update(cosine=V((512, 128), F32), sine=V((512, 128), F32), mask=V((512, 512), BF))
     s.update(p0=V((8, 256, 256), BF), p1=V((8, 256, 512), BF))
@@ -738,12 +758,16 @@
     s.update(dp=V((512, 2048), BF))
     s.update(ga=V((24, 128), F32), gv=V((8, 1024), F32), gg=V((8, 1024), F32), land_a=V((10, 24, 128), F32), land_b=V((10, 24, 128), F32))
     for k in KINDS:
-        for p in range(3):
-            s["land_%s%d" % (k, p)] = V((6,) + half_shape(k, ORDERS[k][:p], ORDERS[k][p]), BF)
+        order = ORDERS[k]
+        for n, (p, chunk) in enumerate(PHASES[k]):
+            s["land_%s%d" % (k, n)] = V((6,) + half_shape(k, order[:p], order[p], chunk), BF)
+    for k in "qkogud":
         s["final_" + k] = V({"q": (2, 32, 256), "k": (2, 32, 256), "o": (2, 2, 16, 256)}.get(k, (2, 48, 256)), F32)
-    for name, n in (("spread", 12), ("gather", 72), ("scatter", 108), ("collect", 20), ("small_a", 10), ("small_b", 10)):
+    phases = 2 * sum(len(p) for p in PHASES.values())
+    for name, n in (("spread", 12), ("collect", 20), ("small_a", 4), ("small_b", 4)):
         s[name + "_send"], s[name + "_recv"] = SEM((n,)), SEM((n,))
-    s.update(spread_local=SEM((2,)), collect_local=SEM((5,)), xsend=SEM((18,)), xrecv=SEM((18,)), xlocal=SEM((18,)))
+    s.update(gather_recv=SEM((phases,)), scatter_recv=SEM((phases,)))
+    s.update(spread_local=SEM((2,)), collect_local=SEM((5,)), xsend=SEM((20,)), xrecv=SEM((20,)), xlocal=SEM((20,)), drained=SEM((4 * len(KINDS),)), fetch=SEM((3,)))
     return s
 
 
@@ -751,116 +775,250 @@
     shapes = scratch()
     S = dict(zip(INPUTS + OUTPUTS + tuple(shapes), refs))
     me = Place()
+    fetch = [pltpu.make_async_copy(S[a], S[b], S["fetch"].at[n]) for n, (a, b) in
+             enumerate((("wq_in", "wqt"), ("wo_in", "wov"), ("wm_in", "wmv")))]
+    for c in fetch:
+        c.start()
     greet(me)
     L = Layer(me, S)
     bufs = {k: S["b" + k] for k in KINDS}
     grads = dict(bufs, q=S["tq"], k=S["tk"])
-    finals = {k: S["final_" + k] for k in KINDS}
-    sp = Spread(me, S["wq_in"], S["wo_in"], S["wm_in"], bufs, S["stage"], S["spread_send"], S["spread_recv"], S["spread_local"])
-    sp.start_attention()
-    arrive = L.tokens_in()
-    for c in arrive:
-        c.start()
-    sp.start_mlp()
-    S["ga"][...] = S["gain_in"][...]
+    finals = {k: S["final_" + k] for k in "qkogud"}
+    sp = Spread(me, S["wqt"], S["wov"], S["wmf"], bufs, S["stage"], S["spread_send"], S["spread_recv"], S["spread_local"])
     ga = SmallSum(me, S["ga"], S["land_a"], S["small_a_send"], S["small_a_recv"])
     gb = SmallSum(me, S["gs"], S["land_b"], S["small_b_send"], S["small_b_recv"])
-    G = {(k, p): Gather(me, k, p, bufs[k], S["gather_send"], S["gather_recv"], (KINDS.index(k) * 3 + p) * 4)
-         for k in KINDS for p in range(3)}
+    C = Collect(me, S["oq"], S["oo"], S["om"], finals, S["collect_send"], S["collect_recv"], S["collect_local"])
+    gathers, scatters, sent, n = {}, {}, S["drained"], 0
+    measure = S["bg"].reshape(1536, 1024)
+    for i, k in enumerate(KINDS):
+        for j, (p, chunk) in enumerate(PHASES[k]):
+            two = lambda name: (S[name].at[2 * n], S[name].at[2 * n + 1])
+            gathers[k, p, chunk] = Gather(me, k, p, chunk, bufs[k], None, measure, sent.at[2 * i + (chunk == 1)], two("gather_recv"))
+            scatters[k, p, chunk] = Scatter(me, k, p, chunk, grads[k], S["land_%s%d" % (k, j)], measure,
+                                            sent.at[12 + 2 * i + (chunk is not None)], two("scatter_recv"), finals[k] if p == 0 else None)
+            n += 1
+
+    def drain(sem, rows):
+        r = ruler(measure, rows)
+        remote(r, r, sem, S["gather_recv"].at[0], me.ring("x", 1)).wait_send()
+
+    def run(table, kinds, p, chunk, acts):
+        for act in acts:
+            for k in kinds:
+                getattr(table[k, p, chunk], act)()
+
+    def G(kinds, p, *acts, chunk=None):
+        run(gathers, kinds, p, chunk, acts)
+
+    def R(kinds, p, *acts, chunk=None):
+        run(scatters, kinds, p, chunk, acts)
+
+    arrive = L.tokens_in()
+    across = L.tokens_across()
+    fetch[0].wait()
+    fetch[1].wait()
+    sp.start_attention()
+    arrive[1].start()
+    arrive[2].start()
+    L.send_piece(0, 0)
+    L.send_piece(0, 1)
+    first = 18 * (me.zlo * 64 + me.dp)
+    wide = jnp.concatenate([S["gain_in"][...].astype(F32), jnp.zeros((1, 238), F32)], axis=1)
+    wide = pltpu.roll(jnp.broadcast_to(wide, (8, 256)), first % 128, 1)[0:1]
+    S["ga"][...] = jnp.zeros((24, 128), F32)
+    S["ga"][pl.ds(first // 128, 1), :] = wide[:, 0:128]
+    S["ga"][pl.ds(first // 128 + 1, 1), :] = wide[:, 128:256]
+    ga.start(0)
+    fetch[2].wait()
+    for t in range(3):
+        S["wmf"][t * 24:(t + 1) * 24, :] = S["wmv"][t].astype(F32)
+    sp.start_mlp()
     sp.wait_attention()
-
-    def gather(rnd):
-        for p in range(3):
-            for act in ("start", "forward", "finish"):
-                for k in rnd:
-                    getattr(G[k, p], act)()
-
-    gather("qko")
+    G(ATT, 0, "start")
+    ga.finish(0)
+    ga.start(1)
+    L.send_piece(0, 2)
+    L.send_piece(0, 3)
     sp.wait_mlp()
-    gather("gud")
-    for c in arrive:
+    G(MLP, 0, "start")
+    G(ATT, 0, "finish")
+    G(ATT, 1, "start")
+    L.send_piece(3, 0)
+    ga.finish(1)
+    ga.start(2)
+    L.acc_o[...] = jnp.zeros((512, 1024), F32)
+    L.acc_d[...] = jnp.zeros((512, 1024), F32)
+    G(MLP, 0, "finish")
+    G(ATT, 1, "forward")
+    G(MLP, 1, "start")
+    ga.finish(2)
+    ga.start(3)
+    for c in arrive[:3]:
         c.wait_recv()
-    across = L.tokens_across()
-    for c in across:
+    for c in across[:3]:
         c.start()
-    for stage in range(4):
-        ga.start(stage)
-        ga.finish(stage)
-    for c in across:
+    G(ATT, 1, "finish")
+    G(ATT, 2, "start")
+    G(MLP, 1, "forward")
+    ga.finish(3)
+    L.gains_rows()
+    for c in across[:3]:
         c.wait()
+    L.tables()
+    L.norm_in()
+    G(ATT, 2, "forward")
+    for i in range(1, 4):
+        L.send_piece(3, i)
+    G(MLP, 1, "finish")
+    G(MLP, 2, "start", chunk=0)
+    G(ATT, 2, "finish")
+    L.project()
+    arrive[3].wait_recv()
+    across[3].start()
+    G(MLP, 2, "forward", chunk=0)
+    G(MLP, 2, "start", chunk=1)
+    L.attend()
+    L.out_project()
+    across[3].wait()
     for c in arrive:
         c.wait_send()
-    for k in KINDS:
-        for p in range(3):
-            G[k, p].drain()
     sp.drain()
-    L.gains_rows()
-    L.tables()
-    L.norm_in()
-    L.project()
-    L.attend()
-    L.out_project()
     L.norm_mid()
-    L.acc_o[...] = jnp.zeros((512, 1024), F32)
-    L.acc_d[...] = jnp.zeros((512, 1024), F32)
-    pl.loop(0, 6)(L.feed_forward)
+    G(MLP, 2, "finish", chunk=0)
+    for i, k in enumerate(KINDS):
+        drain(sent.at[2 * i], 63 * 16 if k in ATT else 3 * 24 + 12 * 24 + 48 * 12)
+
+    @pl.loop(0, 3)
+    def _(c):
+        L.feed_forward(0, c)
+
+        @pl.when(c == 0)
+        def _():
+            G(MLP, 2, "forward", chunk=1)
+
+    R(MLP, 2, "start", chunk=0)
+    G(MLP, 2, "finish", chunk=1)
+    for i in range(3, 6):
+        drain(sent.at[2 * i + 1], 48 * 12)
+
+    @pl.loop(0, 3)
+    def _(c):
+        L.feed_forward(1, c)
+
+    R(MLP, 2, "forward", chunk=0)
+    R(MLP, 2, "start", chunk=1)
     L.send_mid()
     L.norm_mid_back()
+    R(MLP, 2, "finish", chunk=0)
     L.finish_output()
     L.out_back()
-    L.attend_back()
-    L.project_back()
+    R(MLP, 2, "forward", chunk=1)
+    L.swap(17, L.lob, L.lo).start()
+    R("o", 2, "start")
+
+    def between(k):
+        @pl.when(k == 2)
+        def _():
+            R(MLP, 2, "finish", chunk=1)
+            R(MLP, 1, "start")
+
+    L.attend_back(between)
+    L.project_back("q")
+    R("q", 2, "start")
+    R("o", 2, "forward")
+    L.project_back("k")
+    R("k", 2, "start")
     L.send_in()
+    R(MLP, 1, "forward")
     L.finish_input()
+    R("q", 2, "forward")
+    R("k", 2, "forward")
     L.gains_flat()
-    C = Collect(me, S["oq"], S["oo"], S["om"], finals, S["collect_send"], S["collect_recv"], S["collect_local"])
-    R = {(k, p): Scatter(me, k, p, grads[k], S["land_%s%d" % (k, p)], S["scatter_send"], S["scatter_recv"],
-                         (KINDS.index(k) * 3 + p) * 6, finals[k] if p == 0 else None) for k in KINDS for p in range(3)}
-
-    def scatter(rnd):
-        for p in (2, 1, 0):
-            for act in ("start", "forward", "finish", "drain"):
-                for k in rnd:
-                    getattr(R[k, p], act)()
-
-    scatter("gud")
-    for k in "gud":
+    gb.start(0)
+    R(MLP, 1, "finish")
+    R(MLP, 0, "start")
+    R("o", 2, "finish")
+    R("o", 1, "start")
+    gb.finish(0)
+    gb.start(1)
+    R("q", 2, "finish")
+    R("q", 1, "start")
+    R("k", 2, "finish")
+    R("k", 1, "start")
+    R("o", 1, "forward")
+    gb.finish(1)
+    gb.start(2)
+    R(MLP, 0, "finish")
+    for k in MLP:
         C.start(k)
-    for stage in range(4):
-        gb.start(stage)
-        gb.finish(stage)
-    scatter("qko")
+    R("q", 1, "forward")
+    R("k", 1, "forward")
+    L.swap(19, L.igb, L.ig).start()
+    R("o", 1, "finish")
+    R("o", 0, "start")
+    R("q", 1, "finish")
+    R("q", 0, "start")
+    R("k", 1, "finish")
+    R("k", 0, "start")
+    gb.finish(2)
+    gb.start(3)
+    R("o", 0, "finish")
     C.start("o")
+    R("qk", 0, "finish")
     C.start("qk")
+    gb.finish(3)
     for k in ("g", "u", "d", "o", "qk"):
         C.finish(k)
-    for n, src, dst in ((15, L.lob, L.lo), (17, L.igb, L.ig)):
+    for i, k in enumerate(KINDS):
+        if k in ATT:
+            drain(sent.at[12 + 2 * i], 63 * 16)
+        else:
+            drain(sent.at[12 + 2 * i], 15 * 24)
+            drain(sent.at[13 + 2 * i], 96 * 12)
+    for n, src, dst in ((17, L.lob, L.lo), (19, L.igb, L.ig)):
         c = L.swap(n, src, dst)
         c.wait_recv()
         c.wait_send()
 
 
+def finish_kernel(*refs):
+    given, gs, outs, gain_out, held, sem = refs[:5], refs[5], refs[6:11], refs[11], refs[12:17], refs[17]
+    loads = [pltpu.make_async_copy(a, b, sem.at[n]) for n, (a, b) in enumerate(zip(given, held))]
+    stores = [pltpu.make_async_copy(a, b, sem.at[5 + n]) for n, (a, b) in enumerate(zip(held, outs))]
+    for m in loads:
+        m.start()
+    first = 18 * (lax.axis_index("seq") * 64 + lax.axis_index("dp"))
+    wide = jnp.concatenate([gs[pl.ds(first // 128, 1), :], gs[pl.ds(first // 128 + 1, 1), :]], axis=1)
+    wide = pltpu.roll(jnp.broadcast_to(wide, (8, 256)), 256 - first % 128, 1)
+    gain_out[...] = wide[0:1, 0:18]
+    for load, store in zip(loads, stores):
+        load.wait()
+        store.start()
+    for m in stores:
+        m.wait()
+
+
 def shards(layer_input, segments, positions, qkv_weight, out_weight, mlp_weight, gains, cotangent):
-    place = lax.axis_index("seq") * 64 + lax.axis_index("dp")
-    meta = jnp.concatenate([segments, positions, jnp.zeros((6, 256), jnp.int32)], axis=0)
-    wm = jnp.transpose(mlp_weight, (1, 0, 2)).reshape(72, 1024).astype(F32)
-    gain = lax.dynamic_update_slice(jnp.zeros((3072,), F32), gains.astype(F32), (place * 18,)).reshape(24, 128)
-    freqs = THETA_BASE ** (-(jnp.arange(64, dtype=F32) * 2.0) / HEAD)
-    sign = jnp.concatenate([-jnp.ones((64,), F32), jnp.ones((64,), F32)])
-    consts = jnp.stack([jnp.concatenate([freqs, freqs]), sign] + [sign] * 6)
-    vm = pl.BlockSpec(memory_space=pltpu.VMEM)
+    vm, hbm = pl.BlockSpec(memory_space=pltpu.VMEM), pl.BlockSpec(memory_space=pl.ANY)
     shape = jax.ShapeDtypeStruct
     lo, ig, oq, oo, om, gs = pl.pallas_call(
         kernel,
         out_shape=(shape((256, 1024), BF), shape((256, 1024), BF), shape((32, 1024), F32), shape((16, 1024), F32),
                    shape((72, 1024), F32), shape((24, 128), F32)),
-        in_specs=[vm] * len(INPUTS),
-        out_specs=(vm,) * len(OUTPUTS),
+        in_specs=[hbm] * 7 + [vm],
+        out_specs=(hbm,) * 5 + (vm,),
         scratch_shapes=list(scratch().values()),
         compiler_params=pltpu.CompilerParams(collective_id=0, has_side_effects=True, vmem_limit_bytes=VMEM_BYTES),
-    )(layer_input[0], cotangent[0], meta, qkv_weight.T, out_weight, wm, gain, consts)
-    return (lo[None], ig[None], oq.T, oo, jnp.transpose(om.reshape(3, 24, 1024), (1, 0, 2)),
-            lax.dynamic_slice(gs.reshape(3072), (place * 18,), (18,)))
+    )(layer_input[0], cotangent[0], segments, positions, qkv_weight.T, out_weight, jnp.transpose(mlp_weight, (1, 0, 2)), gains.reshape(1, 18))
+    lo, ig, oq, oo, om, gs = pl.pallas_call(
+        finish_kernel,
+        out_shape=(shape((256, 1024), BF), shape((256, 1024), BF), shape((32, 1024), F32), shape((16, 1024), F32),
+                   shape((72, 1024), F32), shape((1, 18), F32)),
+        in_specs=[hbm] * 5 + [vm],
+        out_specs=(hbm,) * 5 + (vm,),
+        scratch_shapes=[V((256, 1024), BF), V((256, 1024), BF), V((32, 1024), F32), V((16, 1024), F32), V((72, 1024), F32), SEM((10,))],
+    )(lo, ig, oq, oo, om, gs)
+    return lo[None], ig[None], oq.T, oo, jnp.transpose(om.reshape(3, 24, 1024), (1, 0, 2)), gs.reshape(18)
 
 
 def solution(mesh):

time: 299 us -> 178 us (0.60)
  Pallas kernels: 287 us -> 177 us
  local copies, waits for them, and re-layouts: 8.24 us -> 0 us
    pallas_call x1, Pallas kernels: 287 us -> 174 us  [shards(): pl.pallas_call(kernel, out_shape=(shape((256, 1024), BF), shape((256, 102...]
    unnamed x23 -> x0, local copies, waits for them, and re-layouts: 6.26 us -> none
    pallas_call x0 -> x1, Pallas kernels: none -> 3.47 us  [shards(): pl.pallas_call(finish_kernel, out_shape=(shape((256, 1024), BF), shape((2...]
where the time goes in v2:
time: 178 us
  Pallas kernels  177 us (99%)
    pallas_call x1, Pallas kernels, shards(): pl.pallas_call(kernel, out_shape=(shape((256, 1024), BF), shape((256, 102...  174 us

profile of v2, /device:TPU:1, one launch (start us, length us, event | category | flops | bytes accessed | tf_op | source)
XLA Modules:
  0.0 178.2 jit_solution(15391845460707728695)
XLA Ops:
  0.6 173.9 %shard_map.127 = (bf16[256,1024]{1,0:T(8,128)(2,1)}, bf16[256,1024]{1,0:T(8,128)(2,1)}, f32[32,1024]{1,0:T(8,128)}, f32[16,1024]{1,0:T(8,128)}, f32[72,1024]{1,0:T(8,128)}, /*index=5*/f32[24,128]{1,0:T(8,128)}) custom-call(bf16[256,1024]{1,0:T(8,128)(2,1)} %bitcast.12, bf16[256,1024]{1,0:T(8,128)(2,1)} %bitcast.13, s32[1,256]{1,0:T(1,128)} %refs_2_.1, ...), custom_call_target="tpu_custom_call" | custom-call | tf_op jit(solution)/shard_map/pallas_call | solution.py:1004
  174.6 3.5 %shard_map.128 = (bf16[256,1024]{1,0:T(8,128)(2,1)}, bf16[256,1024]{1,0:T(8,128)(2,1)}, f32[32,1024]{1,0:T(8,128)}, f32[16,1024]{1,0:T(8,128)}, f32[72,1024]{1,0:T(8,128)}, /*index=5*/f32[1,18]{1,0:T(1,128)}) custom-call(bf16[256,1024]{1,0:T(8,128)(2,1)} %get-tuple-element.18.refs_0_, bf16[256,1024]{1,0:T(8,128)(2,1)} %get-tuple-element.19.refs_1_, ...), custom_call_target="tpu_custom_call" | custom-call | tf_op jit(solution)/shard_map/pallas_call | solution.py:1013

commit v3 on v2

--- a/solution.py
+++ b/solution.py
@@ -514,13 +514,13 @@
             self.cosine[h * 256:(h + 1) * 256] = jnp.cos(angle)
             self.sine[h * 256:(h + 1) * 256] = jnp.sin(angle) * sign
         for q in range(2):
-            seg_q = jnp.broadcast_to(self.seg[q].astype(F32), (128, 256)).T[:, 0:1]
-            for k in range(2):
-                seg_k = self.seg[k].astype(F32)
-                row = lax.broadcasted_iota(jnp.int32, (256, 256), 0) + q * 256
-                col = lax.broadcasted_iota(jnp.int32, (256, 256), 1) + k * 256
-                allowed = (seg_q == seg_k) & (col <= row)
-                self.mask[q * 256:(q + 1) * 256, k * 256:(k + 1) * 256] = jnp.where(allowed, 0.0, MASKED).astype(BF)
+            seg_q = self.seg[q].astype(F32)
+            for k in range(q + 1):
+                seg_k = jnp.broadcast_to(self.seg[k].astype(F32), (128, 256)).T[:, 0:1]
+                key = lax.broadcasted_iota(jnp.int32, (256, 256), 0) + k * 256
+                query = lax.broadcasted_iota(jnp.int32, (256, 256), 1) + q * 256
+                allowed = (seg_q == seg_k) & (key <= query)
+                self.mask[k * 256:(k + 1) * 256, q * 256:(q + 1) * 256] = jnp.where(allowed, 0.0, MASKED).astype(BF)
 
     def norm_in(self):
         gain = self.gv[0:1, :]
@@ -571,11 +571,11 @@
                 keys, values = self.kr[0:n, kcols], self.vl[0:n, kcols]
                 for g in range(2):
                     qcols = pl.ds(pl.multiple_of(k * 256 + g * 128, 128), 128)
-                    s = dot_t(self.qr[rows, qcols], keys)
-                    p = jnp.exp2(s * factor + self.mask[rows, 0:n].astype(F32))
-                    p = (p * (1.0 / jnp.sum(p, axis=-1, keepdims=True))).astype(BF)
+                    s = dot_t(keys, self.qr[rows, qcols])
+                    p = jnp.exp2(s * factor + self.mask[0:n, rows].astype(F32))
+                    p = (p * (1.0 / jnp.sum(p, axis=0, keepdims=True))).astype(BF)
                     (self.p0 if b == 0 else self.p1)[2 * k + g] = p
-                    self.cx[rows, qcols] = dot(p, values).astype(BF)
+                    self.cx[rows, qcols] = dot_c(values, p).T.astype(BF)
 
     def exchange(self, n, chunk, land):
         cols = slice(chunk * 256, (chunk + 1) * 256)
@@ -601,7 +601,7 @@
             self.hid[r] = v
             self.mi[r] = (v * norm_scale(v) * gain).astype(BF)
 
-    def feed_forward(self, j, c):
+    def units(self, j, c):
         wg2, wu2, wd2 = self.mlp[j]
         r = rows_of(c, 256)
         gate = dot_t(self.mi[...], wg2[r])
@@ -612,15 +612,36 @@
         act = (silu * up).astype(BF)
         d_gate = (back * up * sig * (1.0 + gate * (1.0 - sig))).astype(BF)
         d_up = (back * silu).astype(BF)
+        self.acc_d[...] += dot(d_gate, wg2[r]) + dot(d_up, wu2[r])
+        return act, d_gate, d_up
+
+    def unit_grads(self, j, c, act, d_gate, d_up):
+        wg2, wu2, wd2 = self.mlp[j]
+        r = rows_of(c, 256)
         self.acc_o[...] += dot(act, wd2[r])
-        self.acc_d[...] += dot(d_gate, wg2[r]) + dot(d_up, wu2[r])
         wd2[r] = dot_c(act, self.ct[...]).astype(BF)
         wg2[r] = dot_c(d_gate, self.mi[...]).astype(BF)
         wu2[r] = dot_c(d_up, self.mi[...]).astype(BF)
 
+    def held_units(self, c):
+        cols = rows_of(c, 256)
+        upper = pl.ds(pl.multiple_of(1024 + c * 256, 256), 256)
+        return self.da.at[:, cols], self.dc.at[:, cols], self.dp.at[:, upper]
+
+    def feed_forward(self, j, c):
+        self.unit_grads(j, c, *self.units(j, c))
+
+    def feed_forward_first(self, c):
+        for ref, v in zip(self.held_units(c), self.units(1, c)):
+            ref[...] = v
+
+    def feed_forward_rest(self, c):
+        self.unit_grads(1, c, *(ref[...] for ref in self.held_units(c)))
+
     def send_mid(self):
-        self.es[...] = self.acc_d[...].astype(BF)
         for j in range(4):
+            cols = slice(j * 256, (j + 1) * 256)
+            self.es[:, cols] = self.acc_d[:, cols].astype(BF)
             self.exchange(12, j, self.r1).start()
 
     def norm_mid_back(self):
@@ -640,9 +661,11 @@
         total = lax.fori_loop(0, 8, body, jnp.zeros((8, 1024), F32))
         self.gg[1:2, :] = jnp.sum(total, axis=0, keepdims=True)
 
-    def finish_output(self):
+    def send_output(self):
         self.ls[...] = self.acc_o[self.theirs].astype(BF)
         self.share(16, self.ls, self.r0.at[pl.ds(0, 256)]).start()
+
+    def finish_output(self):
         self.share(16, self.ls, self.r0.at[pl.ds(0, 256)]).wait()
         self.lob[...] = (self.acc_o[self.mine] + self.hid[self.mine] + self.r0[0:256].astype(F32)).astype(BF)
 
@@ -650,9 +673,6 @@
         for j in range(4):
             r = slice(j * 256, (j + 1) * 256)
             self.dc[:, r] = dot_t(self.da[...], self.wo2[r]).astype(BF)
-        for j in range(4):
-            r = slice(j * 256, (j + 1) * 256)
-            self.wo2[r] = dot_c(self.cx[:, r], self.da[...]).astype(BF)
 
     def attend_back(self, between):
         scale = HEAD ** -0.5
@@ -660,6 +680,8 @@
 
         def body(k, totals):
             total_q, total_k = totals
+            r = rows_of(k, 256)
+            self.wo2[r] = dot_c(self.cx[:, r], self.da[...]).astype(BF)
             kcols = rows_of(k, 128)
             dk, dv = [0.0, 0.0], [0.0, 0.0]
             for b in range(2):
@@ -671,13 +693,13 @@
                     low = (self.p0 if b == 0 else self.p1)[2 * k + g]
                     dc = self.dc[rows, qcols]
                     p = low.astype(F32)
-                    t = p * dot_t(dc, values)
-                    ds = (t - p * jnp.sum(t, axis=-1, keepdims=True)).astype(BF)
-                    dz = self.unrope(dot(ds, keys) * scale, rows)
+                    t = p * dot_t(values, dc)
+                    ds = (t - p * jnp.sum(t, axis=0, keepdims=True)).astype(BF)
+                    dz = self.unrope(dot_c(keys, ds).T * scale, rows)
                     dq, term = norm_back(dz, self.qp[rows, qcols].astype(F32), gq)
                     self.dp[rows, qcols] = dq.astype(BF)
                     total_q = total_q + fold_rows(term)
-                    pk, pv = dot_c(ds, self.qr[rows, qcols]), dot_c(low, dc)
+                    pk, pv = dot(ds, self.qr[rows, qcols]), dot(low, dc)
                     for j in range(b + 1):
                         part = slice(j * 256, (j + 1) * 256)
                         dk[j] = dk[j] + pk[part]
@@ -751,7 +773,7 @@
     s.update(xa=V((512, 1024), BF), ct=V((512, 1024), BF), seg=V((2, 1, 256), jnp.int32), pos=V((2, 1, 256), jnp.int32), xn=V((512, 1024), BF))
     s.update(qp=V((512, 1024), BF), kp=V((512, 512), BF), qr=V((512, 1024), BF), kr=V((512, 512), BF), vl=V((512, 512), BF))
     s.update(cosine=V((512, 128), F32), sine=V((512, 128), F32), mask=V((512, 512), BF))
-    s.update(p0=V((8, 256, 256), BF), p1=V((8, 256, 512), BF))
+    s.update(p0=V((8, 256, 256), BF), p1=V((8, 512, 256), BF))
     s.update(hid=V((512, 1024), F32), acc_o=V((512, 1024), F32), acc_d=V((512, 1024), F32))
     s.update(r0=V((512, 1024), BF), r1=V((512, 1024), BF))
     s.update(ls=V((256, 1024), BF))
@@ -832,9 +854,9 @@
     fetch[2].wait()
     for t in range(3):
         S["wmf"][t * 24:(t + 1) * 24, :] = S["wmv"][t].astype(F32)
-    sp.start_mlp()
     sp.wait_attention()
     G(ATT, 0, "start")
+    sp.start_mlp()
     ga.finish(0)
     ga.start(1)
     L.send_piece(0, 2)
@@ -849,8 +871,8 @@
     L.acc_o[...] = jnp.zeros((512, 1024), F32)
     L.acc_d[...] = jnp.zeros((512, 1024), F32)
     G(MLP, 0, "finish")
+    G(MLP, 1, "start")
     G(ATT, 1, "forward")
-    G(MLP, 1, "start")
     ga.finish(2)
     ga.start(3)
     for c in arrive[:3]:
@@ -867,17 +889,17 @@
     L.tables()
     L.norm_in()
     G(ATT, 2, "forward")
+    G(MLP, 1, "finish")
+    G(MLP, 2, "start", chunk=0)
     for i in range(1, 4):
         L.send_piece(3, i)
-    G(MLP, 1, "finish")
-    G(MLP, 2, "start", chunk=0)
+    G(MLP, 2, "start", chunk=1)
     G(ATT, 2, "finish")
     L.project()
+    G(MLP, 2, "forward", chunk=0)
+    L.attend()
     arrive[3].wait_recv()
     across[3].start()
-    G(MLP, 2, "forward", chunk=0)
-    G(MLP, 2, "start", chunk=1)
-    L.attend()
     L.out_project()
     across[3].wait()
     for c in arrive:
@@ -903,65 +925,70 @@
 
     @pl.loop(0, 3)
     def _(c):
-        L.feed_forward(1, c)
-
+        L.feed_forward_first(c)
+
+    L.send_mid()
     R(MLP, 2, "forward", chunk=0)
+    pl.loop(0, 3)(L.feed_forward_rest)
     R(MLP, 2, "start", chunk=1)
-    L.send_mid()
     L.norm_mid_back()
+    L.send_output()
     R(MLP, 2, "finish", chunk=0)
-    L.finish_output()
     L.out_back()
     R(MLP, 2, "forward", chunk=1)
-    L.swap(17, L.lob, L.lo).start()
-    R("o", 2, "start")
 
     def between(k):
+        @pl.when(k == 0)
+        def _():
+            L.finish_output()
+            L.swap(17, L.lob, L.lo).start()
+
         @pl.when(k == 2)
         def _():
             R(MLP, 2, "finish", chunk=1)
             R(MLP, 1, "start")
 
     L.attend_back(between)
+    R("o", 2, "start")
     L.project_back("q")
     R("q", 2, "start")
-    R("o", 2, "forward")
+    R(MLP, 1, "forward")
     L.project_back("k")
     R("k", 2, "start")
     L.send_in()
-    R(MLP, 1, "forward")
+    R("o", 2, "forward")
+    R("q", 2, "forward")
     L.finish_input()
-    R("q", 2, "forward")
     R("k", 2, "forward")
     L.gains_flat()
     gb.start(0)
     R(MLP, 1, "finish")
     R(MLP, 0, "start")
+    gb.finish(0)
+    gb.start(1)
     R("o", 2, "finish")
     R("o", 1, "start")
-    gb.finish(0)
-    gb.start(1)
     R("q", 2, "finish")
     R("q", 1, "start")
     R("k", 2, "finish")
     R("k", 1, "start")
-    R("o", 1, "forward")
-    gb.finish(1)
-    gb.start(2)
     R(MLP, 0, "finish")
     for k in MLP:
         C.start(k)
+    gb.finish(1)
+    gb.start(2)
+    R("o", 1, "forward")
     R("q", 1, "forward")
     R("k", 1, "forward")
     L.swap(19, L.igb, L.ig).start()
+    gb.finish(2)
+    gb.start(3)
     R("o", 1, "finish")
     R("o", 0, "start")
     R("q", 1, "finish")
     R("q", 0, "start")
     R("k", 1, "finish")
     R("k", 0, "start")
-    gb.finish(2)
-    gb.start(3)
     R("o", 0, "finish")
     C.start("o")
     R("qk", 0, "finish")

time: 178 us -> 176 us (0.989)
  Pallas kernels: 177 us -> 175 us
    pallas_call x1, Pallas kernels: 174 us -> 171 us  [shards(): pl.pallas_call(kernel, out_shape=(shape((256, 1024), BF), shape((256, 102...]
where the time goes in v3:
time: 176 us
  Pallas kernels  175 us (99%)
    pallas_call x1, Pallas kernels, shards(): pl.pallas_call(kernel, out_shape=(shape((256, 1024), BF), shape((256, 102...  171 us

profile of v3, /device:TPU:1, one launch (start us, length us, event | category | flops | bytes accessed | tf_op | source)
XLA Modules:
  0.0 175.6 jit_solution(6386787543090546192)
XLA Ops:
  0.6 171.3 %shard_map.127 = (bf16[256,1024]{1,0:T(8,128)(2,1)}, bf16[256,1024]{1,0:T(8,128)(2,1)}, f32[32,1024]{1,0:T(8,128)}, f32[16,1024]{1,0:T(8,128)}, f32[72,1024]{1,0:T(8,128)}, /*index=5*/f32[24,128]{1,0:T(8,128)}) custom-call(bf16[256,1024]{1,0:T(8,128)(2,1)} %bitcast.12, bf16[256,1024]{1,0:T(8,128)(2,1)} %bitcast.13, s32[1,256]{1,0:T(1,128)} %refs_2_.1, ...), custom_call_target="tpu_custom_call" | custom-call | tf_op jit(solution)/shard_map/pallas_call | solution.py:1031
  171.9 3.5 %shard_map.128 = (bf16[256,1024]{1,0:T(8,128)(2,1)}, bf16[256,1024]{1,0:T(8,128)(2,1)}, f32[32,1024]{1,0:T(8,128)}, f32[16,1024]{1,0:T(8,128)}, f32[72,1024]{1,0:T(8,128)}, /*index=5*/f32[1,18]{1,0:T(1,128)}) custom-call(bf16[256,1024]{1,0:T(8,128)(2,1)} %get-tuple-element.18.refs_0_, bf16[256,1024]{1,0:T(8,128)(2,1)} %get-tuple-element.19.refs_1_, ...), custom_call_target="tpu_custom_call" | custom-call | tf_op jit(solution)/shard_map/pallas_call | solution.py:1040

commit v4 on v3

--- a/solution.py
+++ b/solution.py
@@ -958,8 +958,8 @@
     L.send_in()
     R("o", 2, "forward")
     R("q", 2, "forward")
+    R("k", 2, "forward")
     L.finish_input()
-    R("k", 2, "forward")
     L.gains_flat()
     gb.start(0)
     R(MLP, 1, "finish")
@@ -980,7 +980,6 @@
     R("o", 1, "forward")
     R("q", 1, "forward")
     R("k", 1, "forward")
-    L.swap(19, L.igb, L.ig).start()
     gb.finish(2)
     gb.start(3)
     R("o", 1, "finish")
@@ -989,6 +988,7 @@
     R("q", 0, "start")
     R("k", 1, "finish")
     R("k", 0, "start")
+    L.swap(19, L.igb, L.ig).start()
     R("o", 0, "finish")
     C.start("o")
     R("qk", 0, "finish")

time: 176 us -> 174 us (0.989)
  Pallas kernels: 175 us -> 173 us
    pallas_call x1, Pallas kernels: 171 us -> 169 us  [shards(): pl.pallas_call(kernel, out_shape=(shape((256, 1024), BF), shape((256, 102...]
where the time goes in v4:
time: 174 us
  Pallas kernels  173 us (99%)
    pallas_call x1, Pallas kernels, shards(): pl.pallas_call(kernel, out_shape=(shape((256, 1024), BF), shape((256, 102...  169 us

profile of v4, /device:TPU:1, one launch (start us, length us, event | category | flops | bytes accessed | tf_op | source)
XLA Modules:
  0.0 173.8 jit_solution(13729711646291241926)
XLA Ops:
  0.6 169.5 %shard_map.127 = (bf16[256,1024]{1,0:T(8,128)(2,1)}, bf16[256,1024]{1,0:T(8,128)(2,1)}, f32[32,1024]{1,0:T(8,128)}, f32[16,1024]{1,0:T(8,128)}, f32[72,1024]{1,0:T(8,128)}, /*index=5*/f32[24,128]{1,0:T(8,128)}) custom-call(bf16[256,1024]{1,0:T(8,128)(2,1)} %bitcast.12, bf16[256,1024]{1,0:T(8,128)(2,1)} %bitcast.13, s32[1,256]{1,0:T(1,128)} %refs_2_.1, ...), custom_call_target="tpu_custom_call" | custom-call | tf_op jit(solution)/shard_map/pallas_call | solution.py:1031
  170.1 3.5 %shard_map.128 = (bf16[256,1024]{1,0:T(8,128)(2,1)}, bf16[256,1024]{1,0:T(8,128)(2,1)}, f32[32,1024]{1,0:T(8,128)}, f32[16,1024]{1,0:T(8,128)}, f32[72,1024]{1,0:T(8,128)}, /*index=5*/f32[1,18]{1,0:T(1,128)}) custom-call(bf16[256,1024]{1,0:T(8,128)(2,1)} %get-tuple-element.18.refs_0_, bf16[256,1024]{1,0:T(8,128)(2,1)} %get-tuple-element.19.refs_1_, ...), custom_call_target="tpu_custom_call" | custom-call | tf_op jit(solution)/shard_map/pallas_call | solution.py:1040
